TPU v7x, 256 devices: a whole 4x4x8 slice. The times are simulated.
256 devices in a mesh: step: 8 (over x, core), seq: 32 (over z, y).
Axes of the slice: x: 4, y: 4, z: 8, core: 2. Of those that a mesh axis runs over, the one named last changes fastest.
Arguments:
- start_latent: float32 [1536, 64], P('seq'), may hold values from -6 to 6
- noise: bfloat16 [16, 1536, 64], P('step', 'seq'), may hold values from -6 to 6
- window_start: int32 [1], replicated, may hold values from 0 to 12
- w_embed: bfloat16 [64, 3072], replicated, may hold values from -0.75 to 0.75
- w_time: bfloat16 [256, 3072], replicated, may hold values from -0.375 to 0.375
- norm_gain: float32 [3072], replicated, may hold values from 0.5 to 2
- w_query: bfloat16 [3072, 2048], P(None, 'step'), may hold values from -0.109375 to 0.109375
- w_key: bfloat16 [3072, 2048], P(None, 'step'), may hold values from -0.109375 to 0.109375
- w_value: bfloat16 [3072, 2048], P(None, 'step'), may hold values from -0.109375 to 0.109375
- query_gain: float32 [128], replicated, may hold values from 1 to 2.5
- key_gain: float32 [128], replicated, may hold values from 1 to 2.5
- w_out: bfloat16 [2048, 3072], P('step'), may hold values from -0.125 to 0.125
- w_final: bfloat16 [3072, 64], replicated, may hold values from -0.109375 to 0.109375
Outputs:
- step_outputs: float32 [16, 1536, 64], P('step', 'seq')
- errors: float32 [16], P('step')
All inputs are finite; a program needn't handle non-finite values.
Results may differ from a plain program's by a relative error of at most 0.0034.
Values may be sent and summed in bfloat16 or wider, within the bound.
A program may use at most 128 MiB of HBM per device.

v0:
```python
import math

import jax
import jax.numpy as jnp
from jax import lax
from jax.experimental import pallas as pl
from jax.experimental.pallas import tpu as pltpu
from jax.sharding import PartitionSpec as P

NSCHED = 28
EPS = 1e-06
SHIFT = 3.0
ETA = 0.5
MESH = pl.DeviceIdType.MESH
F32 = jnp.float32
BF16 = jnp.bfloat16

D = 3072
C = 64
HEAD = 128
LEN = 1536
HALF = LEN // 2
STEPS = 16
ROWS = 48
SEQ = 32
COLS = 8
QBLK = 256
KBLK = 512


def sigma_of(index):
    fraction = 1.0 - index / NSCHED
    return SHIFT * fraction / (1.0 + (SHIFT - 1.0) * fraction)


def chunk_i(n):
    return 2 * lax.rem(n, 4) + lax.div(n, 8)


def chunk_p(n):
    return lax.rem(lax.div(n, 4), 2)


def seq_of(step, part):
    return 2 * step + lax.rem(step + part, 2)


def chunk_block(n):
    return 4 * lax.rem(n, 8) + lax.div(n, 8)


def split(x):
    hi = x.astype(BF16)
    rest = x - hi.astype(F32)
    mid = rest.astype(BF16)
    low = (rest - mid.astype(F32)).astype(BF16)
    return hi, mid, low


def mm(a, b):
    return jnp.dot(a, b, preferred_element_type=F32)


def kernel(
    ws_ref, start_hbm, noise_hbm, gain_hbm, qg_hbm, kg_hbm,
    wembed_hbm, wtime_hbm, wfinal_hbm, wq_hbm, wk_hbm, wv_hbm, wo_hbm,
    out_ref, err_ref,
    start_ref, noise_ref, gain_ref, qg_ref, kg_ref,
    wtime, wall, fold, left, right, wqkv, cdiag, crow,
    delta_ref, coeff_ref,
    zsrc, yin, slab, nsrc, nin, basesrc, basein,
    latents, heads, red, vsrc, mate, psend, gat, zsend, fin0, fin1, first_sums, esrc, ein,
    ztr, kbuf, qbuf, vbuf,
    wsem, ys, yr, zs, zr, cs, cr, ns, nr, bs, br, us, ur, gs, gr, ps, pr, fs, fr, es, er, ms, mr,
):
    i = lax.axis_index("step")
    j = lax.axis_index("seq")
    x = lax.div(i, 2)
    c = lax.rem(i, 2)
    z = lax.div(j, 4)
    y = lax.rem(j, 4)
    s = lax.div(j, 2)
    p = lax.rem(j + s, 2)
    pos = 4 * (2 * c + p) + x
    own_chunk = 8 * lax.rem(y, 2) + z
    half = lax.div(y, 2)
    source_i = chunk_i(own_chunk)
    source_p = chunk_p(own_chunk)
    first_block = chunk_block(pos)
    low_lanes = lax.broadcasted_iota(jnp.int32, (ROWS, 128), 1) < C

    def rows_of(n):
        return pl.ds(pl.multiple_of(n * ROWS, 16), ROWS)

    def push(src, dst, send, recv, to_i, to_j):
        pltpu.make_async_remote_copy(
            src_ref=src, dst_ref=dst, send_sem=send, recv_sem=recv,
            device_id=(to_i, to_j), device_id_type=MESH,
        ).start()

    def await_bytes(like, sem):
        pltpu.make_async_copy(like, like, sem).wait()

    def loop(low, high, fn):
        def body(k, carry):
            fn(k)
            return carry
        lax.fori_loop(low, high, body, 0)

    def each(low, high, fn):
        for k in range(low, high):
            fn(k)

    def group(fn):
        def one(k):
            n = lax.rem(pos + k, STEPS)
            fn(n, chunk_i(n), seq_of(s, chunk_p(n)))
        each(1, STEPS, one)

    zp = latents.at[0]
    zp2 = latents.at[1]

    head = pl.multiple_of(p * HEAD, HEAD)
    pairs = [
        (start_hbm, start_ref), (noise_hbm, noise_ref), (wtime_hbm, wtime), (wembed_hbm, left.at[0:64, :]),
        (gain_hbm, gain_ref), (wembed_hbm, right.at[128:192, :]), (wfinal_hbm, right.at[0:64, :]),
        (wfinal_hbm, right.at[64:128, :]), (wo_hbm.at[pl.ds(head, HEAD), :], left.at[112:240, :]),
        (qg_hbm, qg_ref), (kg_hbm, kg_ref),
    ] + [
        (w.at[:, pl.ds(head, HEAD)], wall.at[:, n * HEAD:(n + 1) * HEAD]) for n, w in enumerate((wq_hbm, wk_hbm, wv_hbm))
    ]
    local = [pltpu.make_async_copy(src, dst, wsem.at[n]) for n, (src, dst) in enumerate(pairs)]
    for copy in local:
        copy.start()

    barrier = pltpu.get_barrier_semaphore()

    def greet(to_i, to_j):
        pl.semaphore_signal(barrier, inc=1, device_id=(to_i, to_j), device_id_type=MESH)

    group(lambda n, ti, tj: greet(ti, tj))
    each(1, 4, lambda k: greet(i, 4 * z + lax.rem(y + k, 4)))
    each(1, 8, lambda k: greet(i, 4 * lax.rem(z + k, 8) + y))
    base_j = [seq_of(2 * i + n, source_p) for n in range(2)]
    base_mine = [jnp.logical_and(source_i == i, tj == j) for tj in base_j]
    from_j = [first_block + 2 * n for n in range(2)]
    from_i = lax.div(s, 2)
    from_mine = [jnp.logical_and(from_i == i, tj == j) for tj in from_j]
    for n in range(2):
        @pl.when(jnp.logical_not(from_mine[n]))
        def _():
            greet(from_i, from_j[n])

    local[0].wait()
    z0 = start_ref[...]
    start_dup = jnp.concatenate([z0, z0], axis=1)
    zsrc[...] = start_dup.astype(BF16)
    yin[y] = start_dup.astype(BF16)
    local[1].wait()
    packed_noise = jnp.concatenate([noise_ref[0], noise_ref[1]], axis=1)
    nsrc[...] = packed_noise
    nin[i] = packed_noise

    first = ws_ref[0]
    index = (lax.broadcasted_iota(jnp.int32, (STEPS, 128), 0) + first).astype(F32)
    sigma_now = sigma_of(index)
    delta = sigma_of(index + 1.0) - sigma_now
    coeff = ETA * jnp.sqrt(-delta)
    delta_ref[...] = delta
    coeff_ref[...] = coeff
    own = sigma_of((jnp.zeros((STEPS, 128), jnp.int32) + (first + s)).astype(F32))
    lane = lax.broadcasted_iota(jnp.int32, (STEPS, 128), 1).astype(F32)
    angle = 1000.0 * own * jnp.exp(-math.log(10000.0) * lane / 128)
    feats = jnp.concatenate([jnp.cos(angle), jnp.sin(angle)], axis=1)
    feats = (feats / (1.0 + jnp.exp(-feats))).astype(BF16)
    right[192:256] = jnp.zeros((64, D), BF16)
    for n in range(2):
        ztr[128 * n + 64:128 * n + 128] = jnp.where(
            lax.broadcasted_iota(jnp.int32, (64, LEN), 0) == 0, 1.0, 0.0).astype(BF16)
    vbuf[C:C + 16] = jnp.ones((16, LEN), BF16)

    for copy in local[3:5]:
        copy.wait()
    local[2].wait()
    temb = mm(feats, wtime[...])

    alone_count = base_mine[0].astype(jnp.int32) + base_mine[1].astype(jnp.int32)
    pl.semaphore_wait(barrier, 15 + 3 + 7 + 2 - alone_count)

    each(1, 4, lambda k: push(zsrc, yin.at[y], ys, yr, i, 4 * z + lax.rem(y + k, 4)))
    each(1, COLS, lambda k: push(nsrc, nin.at[i], ns, nr, lax.rem(i + k, COLS), j))

    emb = left[0:64].astype(F32)
    gain = gain_ref[...]
    for n, part in enumerate(split(jnp.concatenate([emb * gain, temb * gain], axis=0))):
        fold[n * 80:(n + 1) * 80] = part
    for n, part in enumerate(split(temb)):
        left[64 + 16 * n:80 + 16 * n] = part
    t_row = temb[0:1]
    twice_et = 2.0 * jnp.sum(emb * t_row, axis=1, keepdims=True)
    t_square = jnp.sum(t_row * t_row, axis=1, keepdims=True)

    await_bytes(yin.at[0:3], yr)
    slab_now = jnp.where(low_lanes, yin[c].astype(F32), yin[c + 2].astype(F32)).astype(BF16)
    slab[...] = slab_now
    slab_rows = rows_of(8 * c + z)
    zp[slab_rows, :] = slab_now
    each(1, 8, lambda k: push(slab, zp.at[slab_rows, :], zs, zr, i, 4 * lax.rem(z + k, 8) + y))

    for copy in local[5:]:
        copy.wait()
    folded = mm(fold[...], wall[...])
    folded = folded[0:80] + folded[80:160] + folded[160:240]
    both = lax.dot_general(left[...], right[...], (((1,), (1,)), ((), ())), preferred_element_type=F32)
    cdup = both[0:64, 0:128]
    gram = both[0:64, 128:256]
    mout = both[112:240, 0:128]
    lanes64 = lax.broadcasted_iota(jnp.int32, (64, 128), 1)
    diag = jnp.concatenate([jnp.where(lanes64 < C, cdup, 0.0), jnp.where(lanes64 < C, 0.0, cdup)], axis=0)
    for n, part in enumerate(split(diag)):
        cdiag[n * 128:(n + 1) * 128] = part
    crow[...] = (both[64:72, 0:128] + both[80:88, 0:128] + both[96:104, 0:128])

    await_bytes(zp.at[0:7 * ROWS, :], zr)
    core_rows = pl.ds(pl.multiple_of(8 * ROWS * c, 16), 8 * ROWS)
    push(zp.at[core_rows, :], zp.at[core_rows, :], cs, cr, i + 1 - 2 * c, j)

    value_fold = jnp.dot(folded[:, 256:384], mout, precision=lax.Precision.HIGHEST, preferred_element_type=F32)
    wide = jnp.concatenate([folded[:, 0:256], value_fold], axis=1)
    wide = jnp.concatenate([wide, jnp.zeros((48, 384), F32)], axis=0).T
    wide = jnp.concatenate([wide[0:320], jnp.where(lanes64 == C, twice_et, gram)], axis=0)
    whi = wide.astype(BF16)
    wqkv[:, 0:128] = whi
    wqkv[:, 128:256] = (wide - whi.astype(F32)).astype(BF16)
    scale_row = qg_ref[...] * kg_ref[...] * (math.log2(math.e) / math.sqrt(HEAD))
    scale_col = jnp.broadcast_to(scale_row, (128, 128)).T[:, 0:1]

    step_row = lax.broadcasted_iota(jnp.int32, (STEPS, 128), 0)
    coeff_even = jnp.sum(jnp.where(step_row == 2 * i, coeff, 0.0), axis=0, keepdims=True)
    coeff_odd = jnp.sum(jnp.where(step_row == 2 * i + 1, coeff, 0.0), axis=0, keepdims=True)

    def send_base():
        await_bytes(nin.at[0:COLS - 1], nr)

        def noise_of(step_pair):
            both = nin[step_pair].astype(F32)
            turned = pltpu.roll(both, C, 1)
            return jnp.where(low_lanes, both, turned), jnp.where(low_lanes, turned, both)

        base = start_dup
        for pair in range(COLS):
            even, odd = noise_of(pair)
            pair_sum = coeff_ref[2 * pair:2 * pair + 1] * even + coeff_ref[2 * pair + 1:2 * pair + 2] * odd
            base = base + jnp.where(pair < i, pair_sum, 0.0)
        own_even, own_odd = noise_of(i)
        after_even = base + coeff_even * own_even
        after_odd = after_even + coeff_odd * own_odd
        basesrc[0] = base
        basesrc[1] = after_even
        basesrc[2] = after_odd
        for n in range(2):
            @pl.when(base_mine[n])
            def _():
                basein[half] = basesrc[n]

            @pl.when(jnp.logical_not(base_mine[n]))
            def _():
                push(basesrc.at[n], basein.at[half], bs.at[n], br.at[half], source_i, base_j[n])

    def attend(lap):
        packed = latents[lap].T
        zb = jnp.concatenate([packed[0:64], packed[64:128]], axis=1)
        ztr[0:64] = zb
        ztr[128:192] = zb

        def project(n):
            cols = pl.ds(pl.multiple_of(n * KBLK, KBLK), KBLK)
            out = mm(wqkv[...], ztr[:, cols])
            yq, yk, yv, yg = out[0:128], out[128:256], out[256:320], out[320:384]
            mean_square = (jnp.sum(ztr[0:64, cols].astype(F32) * yg, axis=0, keepdims=True) + t_square) * (1.0 / D)
            square = jnp.maximum(mean_square, 0.0) + EPS
            aq = lax.rsqrt(jnp.mean(yq * yq, axis=0, keepdims=True) + EPS * square)
            ak = lax.rsqrt(jnp.mean(yk * yk, axis=0, keepdims=True) + EPS * square)
            qbuf[:, cols] = (yq * aq * scale_col).astype(BF16)
            kbuf[cols, :] = (yk * ak).astype(BF16).T
            vbuf[0:C, cols] = (yv * lax.rsqrt(square)).astype(BF16)

        loop(0, LEN // KBLK, project)

        def send(n):
            @pl.when(n != pos)
            def _():
                push(heads.at[lap, rows_of(n), :], red.at[lap, pos], us.at[lap], ur.at[lap], chunk_i(n), seq_of(s, chunk_p(n)))

        def block_of(block):
            outs = []
            for side in range(2):
                q = qbuf[:, pl.ds(pl.multiple_of(side * HALF + block * QBLK, QBLK), QBLK)]
                acc = jnp.zeros((C + 16, QBLK), F32)
                for m in range(LEN // KBLK):
                    weights = jnp.exp2(mm(kbuf[m * KBLK:(m + 1) * KBLK], q))
                    acc = acc + mm(vbuf[:, m * KBLK:(m + 1) * KBLK], weights.astype(BF16))
                outs.append(acc[0:C] / acc[C:C + 1])
            done = pl.ds(pl.multiple_of(block * QBLK, QBLK), QBLK)
            heads[lap, done, :] = jnp.concatenate(outs, axis=0).astype(BF16).T
            each(0, 5, lambda m: send(5 * block + m))

            @pl.when(block == 2)
            def _():
                send(15)

        loop(0, 3, block_of)

    def reduce_heads(lap):
        chunk = rows_of(pos)
        red[lap, pos] = heads[lap, chunk, :]
        latent = latents[lap, chunk, :]
        total = mm(jnp.concatenate([latent, latent, latent], axis=1), cdiag[...]) + crow[0:1]
        await_bytes(red.at[lap, 0:STEPS - 1], ur.at[lap])
        for h in range(STEPS):
            total = total + red[lap, h].astype(F32)
        total = total.astype(BF16)
        vsrc[lap] = total
        return total

    first_i = lax.div(s, 2)

    def owner_case(k):
        to_i = k // 2
        to_j = first_block + 2 * (k % 2)
        mine = jnp.logical_and(to_i == i, to_j == j)
        wanted = to_i >= first_i
        return to_i, to_j, jnp.logical_and(wanted, mine), jnp.logical_and(wanted, jnp.logical_not(mine))

    def to_owners(src, dst, n):
        def one(k):
            to_i, to_j, here, there = owner_case(k)

            @pl.when(here)
            def _():
                dst[s] = src[...]

            @pl.when(there)
            def _():
                push(src, dst.at[s], fs.at[n, k], fr.at[n], to_i, to_j)
        each(0, 16, one)

    def owners_sent(src, n):
        def one(k):
            @pl.when(owner_case(k)[3])
            def _():
                await_bytes(src, fs.at[n, k])
        each(0, 16, one)

    alone = jnp.logical_and(own_chunk == pos, first_i <= i)

    def owner_sums(dst, n):
        for pair in range(COLS):
            for own in range(2):
                @pl.when(jnp.logical_and(i == pair, alone == (own == 1)))
                def _():
                    await_bytes(dst.at[0:2 * pair + 2 - own], fr.at[n])
        even = jnp.zeros((ROWS, 128), F32)
        odd = even
        for k in range(STEPS):
            later = delta_ref[k:k + 1] * dst[k].astype(F32)
            even = even + jnp.where(k <= 2 * i, later, 0.0)
            odd = odd + jnp.where(k == 2 * i + 1, later, 0.0)
        return even, even + odd

    chunk = rows_of(pos)
    await_bytes(zp.at[0:8 * ROWS, :], cr)

    def iteration(lap):
        attend(lap)

        @pl.when(lap == 0)
        def _():
            send_base()

        @pl.when(lap == 1)
        def _():
            first_sums[0], first_sums[1] = owner_sums(fin0, 0)

        velocity = reduce_heads(lap)

        @pl.when(lap == 0)
        def _():
            even = lax.rem(s, 2) == 0
            partner = seq_of(s + 1 - 2 * lax.rem(s, 2), p)
            push(vsrc.at[0], mate, ms, mr, i, partner)
            delta_low = jnp.sum(jnp.where(step_row == 2 * z, delta, 0.0), axis=0, keepdims=True)
            delta_high = jnp.sum(jnp.where(step_row == 2 * z + 1, delta, 0.0), axis=0, keepdims=True)
            mine = vsrc[0].astype(F32)
            await_bytes(mate, mr)
            other = mate[...].astype(F32)
            low = delta_low * jnp.where(even, mine, other)
            pair = (low + delta_high * jnp.where(even, other, mine)).astype(BF16)
            gat[z] = pair
            psend[...] = pair
            each(1, 8, lambda k: push(psend, gat.at[z], gs, gr, i, 4 * lax.rem(z + k, 8) + y))
            for n in range(2):
                @pl.when(jnp.logical_not(from_mine[n]))
                def _():
                    await_bytes(basein.at[n], br.at[n])
            latent = jnp.where(low_lanes, basein[0], basein[1]) + jnp.where(even, 0.0, low)
            await_bytes(gat.at[0:7], gr)
            for n in range(8):
                latent = latent + jnp.where(n < z, gat[n].astype(F32), 0.0)
            latent = latent.astype(BF16)
            zsend[...] = latent
            zp2[chunk, :] = latent
            group(lambda n, ti, tj: push(zsend, zp2.at[chunk, :], ps, pr, ti, tj))
            to_owners(vsrc.at[0], fin0, 0)
            await_bytes(zp2.at[0:15 * ROWS, :], pr)

    loop(0, 2, iteration)
    to_owners(vsrc.at[1], fin1, 1)

    keep = low_lanes == (half == 0)
    even, odd = owner_sums(fin1, 1)
    change_even = even - first_sums[0]
    change_odd = odd - first_sums[1]
    row = lax.broadcasted_iota(jnp.int32, (2, 128), 0)
    sum_even = jnp.sum(jnp.where(keep, change_even * change_even, 0.0), axis=0, keepdims=True)
    sum_odd = jnp.sum(jnp.where(keep, change_odd * change_odd, 0.0), axis=0, keepdims=True)
    partial = jnp.where(row == 0, sum_even, sum_odd)
    esrc[0] = partial
    ein[z] = partial
    each(1, 8, lambda k: push(esrc.at[0], ein.at[z], es.at[0], er.at[0], i, 4 * lax.rem(z + k, 8) + y))
    for n, total in enumerate((basesrc[1] + even, basesrc[2] + odd)):
        out_ref[n] = jnp.where(half == 0, total, pltpu.roll(total, C, 1))[:, 0:C]
    await_bytes(ein.at[0:7], er.at[0])
    total = ein[0]
    for n in range(1, 8):
        total = total + ein[n]
    esrc[1] = total
    ein[8 + y] = total
    each(1, 4, lambda k: push(esrc.at[1], ein.at[8 + y], es.at[1], er.at[1], i, 4 * z + lax.rem(y + k, 4)))
    await_bytes(ein.at[8:11], er.at[1])
    total = (ein[8] + ein[9]) + (ein[10] + ein[11])
    total = total * (1.0 / (LEN * C))
    err_ref[0] = jnp.sum(total[0:1] / (coeff_even * coeff_even))
    err_ref[1] = jnp.sum(total[1:2] / (coeff_odd * coeff_odd))

    await_bytes(ein.at[0:7], es.at[0])
    await_bytes(ein.at[8:11], es.at[1])
    await_bytes(mate, ms)
    await_bytes(red.at[0, 0:STEPS - 1], us.at[0])
    await_bytes(red.at[1, 0:STEPS - 1], us.at[1])
    await_bytes(gat.at[0:7], gs)
    await_bytes(zp2.at[0:15 * ROWS, :], ps)
    owners_sent(vsrc.at[0], 0)
    owners_sent(vsrc.at[1], 1)
    await_bytes(yin.at[0:3], ys)
    await_bytes(nin.at[0:COLS - 1], ns)
    await_bytes(zp.at[0:7 * ROWS, :], zs)
    await_bytes(zp.at[0:8 * ROWS, :], cs)
    for n in range(2):
        @pl.when(jnp.logical_not(base_mine[n]))
        def _():
            await_bytes(basesrc.at[n], bs.at[n])


def per_device(
    start_latent, noise, window_start, w_embed, w_time, norm_gain, w_query, w_key, w_value, query_gain, key_gain, w_out, w_final,
):
    vmem = pl.BlockSpec(memory_space=pltpu.VMEM)
    hbm = pl.BlockSpec(memory_space=pltpu.HBM)
    smem = pl.BlockSpec(memory_space=pltpu.SMEM)
    dma = pltpu.SemaphoreType.DMA
    out, errors = pl.pallas_call(
        kernel,
        out_shape=(
            pltpu.VMEM((2, ROWS, C), F32),
            pltpu.SMEM((2,), F32),
        ),
        in_specs=[smem] + [hbm] * 12,
        out_specs=(vmem, smem),
        scratch_shapes=[
            pltpu.VMEM((ROWS, C), F32),
            pltpu.VMEM((2, ROWS, C), BF16),
            pltpu.VMEM((1, D), F32),
            pltpu.VMEM((1, HEAD), F32),
            pltpu.VMEM((1, HEAD), F32),
            pltpu.VMEM((256, D), BF16),
            pltpu.VMEM((D, 3 * HEAD), BF16),
            pltpu.VMEM((240, D), BF16),
            pltpu.VMEM((240, D), BF16),
            pltpu.VMEM((256, D), BF16),
            pltpu.VMEM((384, 256), BF16),
            pltpu.VMEM((384, 128), BF16),
            pltpu.VMEM((8, 128), F32),
            pltpu.VMEM((STEPS, 128), F32),
            pltpu.VMEM((STEPS, 128), F32),
            pltpu.VMEM((ROWS, 128), BF16),
            pltpu.VMEM((4, ROWS, 128), BF16),
            pltpu.VMEM((ROWS, 128), BF16),
            pltpu.VMEM((ROWS, 128), BF16),
            pltpu.VMEM((COLS, ROWS, 128), BF16),
            pltpu.VMEM((3, ROWS, 128), F32),
            pltpu.VMEM((2, ROWS, 128), F32),
            pltpu.VMEM((2, HALF, 128), BF16),
            pltpu.VMEM((2, HALF, 128), BF16),
            pltpu.VMEM((2, STEPS, ROWS, 128), BF16),
            pltpu.VMEM((2, ROWS, 128), BF16),
            pltpu.VMEM((ROWS, 128), BF16),
            pltpu.VMEM((ROWS, 128), BF16),
            pltpu.VMEM((8, ROWS, 128), BF16),
            pltpu.VMEM((ROWS, 128), BF16),
            pltpu.VMEM((STEPS, ROWS, 128), BF16),
            pltpu.VMEM((STEPS, ROWS, 128), BF16),
            pltpu.VMEM((2, ROWS, 128), F32),
            pltpu.VMEM((2, 2, 128), F32),
            pltpu.VMEM((12, 2, 128), F32),
            pltpu.VMEM((256, LEN), BF16),
            pltpu.VMEM((LEN, HEAD), BF16),
            pltpu.VMEM((HEAD, LEN), BF16),
            pltpu.VMEM((C + 16, LEN), BF16),
            dma((14,)),
            dma, dma, dma, dma, dma, dma, dma, dma, dma((2,)), dma((2,)),
            dma((2,)), dma((2,)), dma, dma, dma, dma, dma((2, STEPS)), dma((2,)), dma((2,)), dma((2,)), dma, dma,
        ],
        compiler_params=pltpu.CompilerParams(
            collective_id=0, has_side_effects=True, vmem_limit_bytes=56 * 1024 * 1024),
    )(
        window_start, start_latent, noise, norm_gain.reshape(1, D), query_gain.reshape(1, HEAD), key_gain.reshape(1, HEAD),
        w_embed, w_time, w_final.T, w_query, w_key, w_value, w_out,
    )
    return out, errors


def solution(mesh):
    return jax.shard_map(
        per_device,
        mesh=mesh,
        in_specs=(
            P("seq", None), P("step", "seq", None), P(), P(), P(), P(),
            P(None, "step"), P(None, "step"), P(None, "step"), P(), P(), P("step", None), P(),
        ),
        out_specs=(P("step", "seq", None), P("step")),
        check_vma=False,
    )
```

profile of v0, /device:TPU:4, one launch (start us, length us, event | category | flops | bytes accessed | tf_op | source)
XLA Modules:
  0.0 81.1 jit_solution(6523752311047521603)
XLA Ops:
  1.3 78.7 %shard_map.140 = (f32[2,48,64]{2,1,0:T(8,128)S(1)}, f32[2]{0:T(128)S(4)}) custom-call(s32[1]{0:T(128)S(6)} %copy.19.ws_ref, f32[48,64]{1,0:T(8,128)} %start_hbm.1, bf16[2,48,64]{2,1,0:T(8,128)(2,1)} %noise_hbm.1, f32[1,3072]{1,0:T(1,128)} %bitcast.5, f32[1,128]{1,0:T(1,128)} %bitcast.6, f32[1,128]{1,0:T(1,128)} %bitcast.7, bf16[64,3072]{1,0:T(8,128)(2,1)} %wembed_hbm.1, ...), custom_call_target="tpu_custom_call" | custom-call | tf_op jit(solution)/shard_map/pallas_call | solution.py:472
  79.9 0.6 copy.17
  80.6 0.5 copy.18
where the time goes:
time: 82.2 us; the launch traced here: 81.1 us
  Pallas kernels  78.7 us (96%)
  between operations  1.29 us (2%)
  local copies, waits for them, and re-layouts  1.14 us (1%)
    pallas_call x1, Pallas kernels, per_device(): pl.pallas_call(kernel, out_shape=(pltpu.VMEM((2, ROWS, C), F32), pltpu.SM...  78.7 us

commit v1 on v0

--- a/solution.py
+++ b/solution.py
@@ -69,7 +69,7 @@
     wtime, wall, fold, left, right, wqkv, cdiag, crow,
     delta_ref, coeff_ref,
     zsrc, yin, slab, nsrc, nin, basesrc, basein,
-    latents, heads, red, vsrc, mate, psend, gat, zsend, fin0, fin1, first_sums, esrc, ein,
+    latents, heads, red, vsrc, vpack, mate, psend, gat, zsend, fin0, fin1, first_sums, esrc, ein,
     ztr, kbuf, qbuf, vbuf,
     wsem, ys, yr, zs, zr, cs, cr, ns, nr, bs, br, us, ur, gs, gr, ps, pr, fs, fr, es, er, ms, mr,
 ):
@@ -90,7 +90,7 @@
     low_lanes = lax.broadcasted_iota(jnp.int32, (ROWS, 128), 1) < C
 
     def rows_of(n):
-        return pl.ds(pl.multiple_of(n * ROWS, 16), ROWS)
+        return pl.ds(pl.multiple_of(n * 16, 16), 16)
 
     def push(src, dst, send, recv, to_i, to_j):
         pltpu.make_async_remote_copy(
@@ -188,7 +188,6 @@
     pl.semaphore_wait(barrier, 15 + 3 + 7 + 2 - alone_count)
 
     each(1, 4, lambda k: push(zsrc, yin.at[y], ys, yr, i, 4 * z + lax.rem(y + k, 4)))
-    each(1, COLS, lambda k: push(nsrc, nin.at[i], ns, nr, lax.rem(i + k, COLS), j))
 
     emb = left[0:64].astype(F32)
     gain = gain_ref[...]
@@ -201,11 +200,13 @@
     t_square = jnp.sum(t_row * t_row, axis=1, keepdims=True)
 
     await_bytes(yin.at[0:3], yr)
-    slab_now = jnp.where(low_lanes, yin[c].astype(F32), yin[c + 2].astype(F32)).astype(BF16)
+    slab_now = jnp.where(low_lanes, yin[c].astype(F32), yin[c + 2].astype(F32)).reshape(3, 16, 128).astype(BF16)
     slab[...] = slab_now
     slab_rows = rows_of(8 * c + z)
-    zp[slab_rows, :] = slab_now
-    each(1, 8, lambda k: push(slab, zp.at[slab_rows, :], zs, zr, i, 4 * lax.rem(z + k, 8) + y))
+    zp[:, slab_rows, :] = slab_now
+    each(1, 8, lambda k: push(slab, zp.at[:, slab_rows, :], zs, zr, i, 4 * lax.rem(z + k, 8) + y))
+
+    each(1, COLS, lambda k: push(nsrc, nin.at[i], ns, nr, lax.rem(i + k, COLS), j))
 
     for copy in local[5:]:
         copy.wait()
@@ -221,9 +222,9 @@
         cdiag[n * 128:(n + 1) * 128] = part
     crow[...] = (both[64:72, 0:128] + both[80:88, 0:128] + both[96:104, 0:128])
 
-    await_bytes(zp.at[0:7 * ROWS, :], zr)
-    core_rows = pl.ds(pl.multiple_of(8 * ROWS * c, 16), 8 * ROWS)
-    push(zp.at[core_rows, :], zp.at[core_rows, :], cs, cr, i + 1 - 2 * c, j)
+    await_bytes(zp.at[:, 0:7 * 16, :], zr)
+    core_rows = pl.ds(pl.multiple_of(128 * c, 128), 128)
+    push(zp.at[:, core_rows, :], zp.at[:, core_rows, :], cs, cr, i + 1 - 2 * c, j)
 
     value_fold = jnp.dot(folded[:, 256:384], mout, precision=lax.Precision.HIGHEST, preferred_element_type=F32)
     wide = jnp.concatenate([folded[:, 0:256], value_fold], axis=1)
@@ -268,7 +269,7 @@
                 push(basesrc.at[n], basein.at[half], bs.at[n], br.at[half], source_i, base_j[n])
 
     def attend(lap):
-        packed = latents[lap].T
+        packed = latents[lap].reshape(HALF, 128).T
         zb = jnp.concatenate([packed[0:64], packed[64:128]], axis=1)
         ztr[0:64] = zb
         ztr[128:192] = zb
@@ -287,11 +288,6 @@
 
         loop(0, LEN // KBLK, project)
 
-        def send(n):
-            @pl.when(n != pos)
-            def _():
-                push(heads.at[lap, rows_of(n), :], red.at[lap, pos], us.at[lap], ur.at[lap], chunk_i(n), seq_of(s, chunk_p(n)))
-
         def block_of(block):
             outs = []
             for side in range(2):
@@ -301,27 +297,29 @@
                     weights = jnp.exp2(mm(kbuf[m * KBLK:(m + 1) * KBLK], q))
                     acc = acc + mm(vbuf[:, m * KBLK:(m + 1) * KBLK], weights.astype(BF16))
                 outs.append(acc[0:C] / acc[C:C + 1])
-            done = pl.ds(pl.multiple_of(block * QBLK, QBLK), QBLK)
-            heads[lap, done, :] = jnp.concatenate(outs, axis=0).astype(BF16).T
-            each(0, 5, lambda m: send(5 * block + m))
-
-            @pl.when(block == 2)
-            def _():
-                send(15)
+            heads[lap, block] = jnp.concatenate(outs, axis=0).astype(BF16).T
+            group(lambda n, ti, tj: push(
+                heads.at[lap, block, rows_of(n), :], red.at[lap, pos, block], us.at[lap], ur.at[lap], ti, tj))
 
         loop(0, 3, block_of)
 
     def reduce_heads(lap):
         chunk = rows_of(pos)
-        red[lap, pos] = heads[lap, chunk, :]
-        latent = latents[lap, chunk, :]
+        red[lap, pos] = heads[lap, :, chunk, :]
+        latent = latents[lap, :, chunk, :].reshape(ROWS, 128)
         total = mm(jnp.concatenate([latent, latent, latent], axis=1), cdiag[...]) + crow[0:1]
         await_bytes(red.at[lap, 0:STEPS - 1], ur.at[lap])
         for h in range(STEPS):
-            total = total + red[lap, h].astype(F32)
-        total = total.astype(BF16)
-        vsrc[lap] = total
-        return total
+            total = total + red[lap, h].astype(F32).reshape(ROWS, 128)
+        vsrc[lap] = total.astype(BF16)
+        low = low_lanes[0:16]
+        parts = [total[0:16], total[16:32], total[32:48]]
+        turned = [pltpu.roll(part, C, 1) for part in parts]
+        for side, (first_part, second_part, third_part) in enumerate((
+            (parts[0], turned[1], parts[2]), (turned[0], parts[1], turned[2]),
+        )):
+            vpack[lap, side, 0:16] = jnp.where(low, first_part, second_part).astype(BF16)
+            vpack[lap, side, 16:32] = jnp.where(low, third_part, 0.0).astype(BF16)
 
     first_i = lax.div(s, 2)
 
@@ -338,18 +336,18 @@
 
             @pl.when(here)
             def _():
-                dst[s] = src[...]
+                dst[s] = src[k % 2]
 
             @pl.when(there)
             def _():
-                push(src, dst.at[s], fs.at[n, k], fr.at[n], to_i, to_j)
+                push(src.at[k % 2], dst.at[s], fs.at[n, k], fr.at[n], to_i, to_j)
         each(0, 16, one)
 
     def owners_sent(src, n):
         def one(k):
             @pl.when(owner_case(k)[3])
             def _():
-                await_bytes(src, fs.at[n, k])
+                await_bytes(src.at[k % 2], fs.at[n, k])
         each(0, 16, one)
 
     alone = jnp.logical_and(own_chunk == pos, first_i <= i)
@@ -360,7 +358,7 @@
                 @pl.when(jnp.logical_and(i == pair, alone == (own == 1)))
                 def _():
                     await_bytes(dst.at[0:2 * pair + 2 - own], fr.at[n])
-        even = jnp.zeros((ROWS, 128), F32)
+        even = jnp.zeros((32, 128), F32)
         odd = even
         for k in range(STEPS):
             later = delta_ref[k:k + 1] * dst[k].astype(F32)
@@ -369,7 +367,7 @@
         return even, even + odd
 
     chunk = rows_of(pos)
-    await_bytes(zp.at[0:8 * ROWS, :], cr)
+    await_bytes(zp.at[:, 0:128, :], cr)
 
     def iteration(lap):
         attend(lap)
@@ -382,7 +380,7 @@
         def _():
             first_sums[0], first_sums[1] = owner_sums(fin0, 0)
 
-        velocity = reduce_heads(lap)
+        reduce_heads(lap)
 
         @pl.when(lap == 0)
         def _():
@@ -407,29 +405,32 @@
             await_bytes(gat.at[0:7], gr)
             for n in range(8):
                 latent = latent + jnp.where(n < z, gat[n].astype(F32), 0.0)
-            latent = latent.astype(BF16)
+            latent = latent.reshape(3, 16, 128).astype(BF16)
             zsend[...] = latent
-            zp2[chunk, :] = latent
-            group(lambda n, ti, tj: push(zsend, zp2.at[chunk, :], ps, pr, ti, tj))
-            to_owners(vsrc.at[0], fin0, 0)
-            await_bytes(zp2.at[0:15 * ROWS, :], pr)
+            zp2[:, chunk, :] = latent
+            group(lambda n, ti, tj: push(zsend, zp2.at[:, chunk, :], ps, pr, ti, tj))
+            to_owners(vpack.at[0], fin0, 0)
+            await_bytes(zp2.at[:, 0:15 * 16, :], pr)
 
     loop(0, 2, iteration)
-    to_owners(vsrc.at[1], fin1, 1)
-
-    keep = low_lanes == (half == 0)
+    to_owners(vpack.at[1], fin1, 1)
+
     even, odd = owner_sums(fin1, 1)
     change_even = even - first_sums[0]
     change_odd = odd - first_sums[1]
+
+    def unpack(x):
+        return jnp.concatenate([x[0:16], pltpu.roll(x[0:16], C, 1), x[16:32]], axis=0)
+
     row = lax.broadcasted_iota(jnp.int32, (2, 128), 0)
-    sum_even = jnp.sum(jnp.where(keep, change_even * change_even, 0.0), axis=0, keepdims=True)
-    sum_odd = jnp.sum(jnp.where(keep, change_odd * change_odd, 0.0), axis=0, keepdims=True)
+    sum_even = jnp.sum(change_even * change_even, axis=0, keepdims=True)
+    sum_odd = jnp.sum(change_odd * change_odd, axis=0, keepdims=True)
     partial = jnp.where(row == 0, sum_even, sum_odd)
     esrc[0] = partial
     ein[z] = partial
     each(1, 8, lambda k: push(esrc.at[0], ein.at[z], es.at[0], er.at[0], i, 4 * lax.rem(z + k, 8) + y))
-    for n, total in enumerate((basesrc[1] + even, basesrc[2] + odd)):
-        out_ref[n] = jnp.where(half == 0, total, pltpu.roll(total, C, 1))[:, 0:C]
+    for n, total in enumerate((basesrc[1] + unpack(even), basesrc[2] + unpack(odd))):
+        out_ref[n] = total[:, 0:C]
     await_bytes(ein.at[0:7], er.at[0])
     total = ein[0]
     for n in range(1, 8):
@@ -449,13 +450,13 @@
     await_bytes(red.at[0, 0:STEPS - 1], us.at[0])
     await_bytes(red.at[1, 0:STEPS - 1], us.at[1])
     await_bytes(gat.at[0:7], gs)
-    await_bytes(zp2.at[0:15 * ROWS, :], ps)
-    owners_sent(vsrc.at[0], 0)
-    owners_sent(vsrc.at[1], 1)
+    await_bytes(zp2.at[:, 0:15 * 16, :], ps)
+    owners_sent(vpack.at[0], 0)
+    owners_sent(vpack.at[1], 1)
     await_bytes(yin.at[0:3], ys)
     await_bytes(nin.at[0:COLS - 1], ns)
-    await_bytes(zp.at[0:7 * ROWS, :], zs)
-    await_bytes(zp.at[0:8 * ROWS, :], cs)
+    await_bytes(zp.at[:, 0:7 * 16, :], zs)
+    await_bytes(zp.at[:, 0:128, :], cs)
     for n in range(2):
         @pl.when(jnp.logical_not(base_mine[n]))
         def _():
@@ -495,22 +496,23 @@
             pltpu.VMEM((STEPS, 128), F32),
             pltpu.VMEM((ROWS, 128), BF16),
             pltpu.VMEM((4, ROWS, 128), BF16),
-            pltpu.VMEM((ROWS, 128), BF16),
+            pltpu.VMEM((3, 16, 128), BF16),
             pltpu.VMEM((ROWS, 128), BF16),
             pltpu.VMEM((COLS, ROWS, 128), BF16),
             pltpu.VMEM((3, ROWS, 128), F32),
             pltpu.VMEM((2, ROWS, 128), F32),
-            pltpu.VMEM((2, HALF, 128), BF16),
-            pltpu.VMEM((2, HALF, 128), BF16),
-            pltpu.VMEM((2, STEPS, ROWS, 128), BF16),
+            pltpu.VMEM((2, 3, QBLK, 128), BF16),
+            pltpu.VMEM((2, 3, QBLK, 128), BF16),
+            pltpu.VMEM((2, STEPS, 3, 16, 128), BF16),
             pltpu.VMEM((2, ROWS, 128), BF16),
+            pltpu.VMEM((2, 2, 32, 128), BF16),
             pltpu.VMEM((ROWS, 128), BF16),
             pltpu.VMEM((ROWS, 128), BF16),
             pltpu.VMEM((8, ROWS, 128), BF16),
-            pltpu.VMEM((ROWS, 128), BF16),
-            pltpu.VMEM((STEPS, ROWS, 128), BF16),
-            pltpu.VMEM((STEPS, ROWS, 128), BF16),
-            pltpu.VMEM((2, ROWS, 128), F32),
+            pltpu.VMEM((3, 16, 128), BF16),
+            pltpu.VMEM((STEPS, 32, 128), BF16),
+            pltpu.VMEM((STEPS, 32, 128), BF16),
+            pltpu.VMEM((2, 32, 128), F32),
             pltpu.VMEM((2, 2, 128), F32),
             pltpu.VMEM((12, 2, 128), F32),
             pltpu.VMEM((256, LEN), BF16),

time: 82.2 us -> 78.5 us (0.955)
  Pallas kernels: 78.7 us -> 75.6 us
    pallas_call x1, Pallas kernels: 78.7 us -> 75.6 us  [per_device(): pl.pallas_call(kernel, out_shape=(pltpu.VMEM((2, ROWS, C), F32), pltpu.SM...]
where the time goes in v1:
time: 78.5 us; the launch traced here: 78 us
  Pallas kernels  75.6 us (96%)
  between operations  1.29 us (2%)
  local copies, waits for them, and re-layouts  1.14 us (1%)
    pallas_call x1, Pallas kernels, per_device(): pl.pallas_call(kernel, out_shape=(pltpu.VMEM((2, ROWS, C), F32), pltpu.SM...  75.6 us

profile of v1, /device:TPU:4, one launch (start us, length us, event | category | flops | bytes accessed | tf_op | source)
XLA Modules:
  0.0 78.0 jit_solution(7085205330982289661)
XLA Ops:
  1.3 75.6 %shard_map.140 = (f32[2,48,64]{2,1,0:T(8,128)S(1)}, f32[2]{0:T(128)S(4)}) custom-call(s32[1]{0:T(128)S(6)} %copy.19.ws_ref, f32[48,64]{1,0:T(8,128)} %start_hbm.1, bf16[2,48,64]{2,1,0:T(8,128)(2,1)} %noise_hbm.1, f32[1,3072]{1,0:T(1,128)} %bitcast.5, f32[1,128]{1,0:T(1,128)} %bitcast.6, f32[1,128]{1,0:T(1,128)} %bitcast.7, bf16[64,3072]{1,0:T(8,128)(2,1)} %wembed_hbm.1, ...), custom_call_target="tpu_custom_call" | custom-call | tf_op jit(solution)/shard_map/pallas_call | solution.py:473
  76.9 0.6 copy.17
  77.5 0.5 copy.18

commit v2 on v1

--- a/solution.py
+++ b/solution.py
@@ -101,12 +101,6 @@
     def await_bytes(like, sem):
         pltpu.make_async_copy(like, like, sem).wait()
 
-    def loop(low, high, fn):
-        def body(k, carry):
-            fn(k)
-            return carry
-        lax.fori_loop(low, high, body, 0)
-
     def each(low, high, fn):
         for k in range(low, high):
             fn(k)
@@ -118,7 +112,6 @@
         each(1, STEPS, one)
 
     zp = latents.at[0]
-    zp2 = latents.at[1]
 
     head = pl.multiple_of(p * HEAD, HEAD)
     pairs = [
@@ -160,6 +153,11 @@
     packed_noise = jnp.concatenate([noise_ref[0], noise_ref[1]], axis=1)
     nsrc[...] = packed_noise
     nin[i] = packed_noise
+
+    alone_count = base_mine[0].astype(jnp.int32) + base_mine[1].astype(jnp.int32)
+    pl.semaphore_wait(barrier, 15 + 3 + 7 + 2 - alone_count)
+
+    each(1, 4, lambda k: push(zsrc, yin.at[y], ys, yr, i, 4 * z + lax.rem(y + k, 4)))
 
     first = ws_ref[0]
     index = (lax.broadcasted_iota(jnp.int32, (STEPS, 128), 0) + first).astype(F32)
@@ -176,18 +174,13 @@
     right[192:256] = jnp.zeros((64, D), BF16)
     for n in range(2):
         ztr[128 * n + 64:128 * n + 128] = jnp.where(
-            lax.broadcasted_iota(jnp.int32, (64, LEN), 0) == 0, 1.0, 0.0).astype(BF16)
+            lax.broadcasted_iota(jnp.int32, (64, KBLK), 0) == 0, 1.0, 0.0).astype(BF16)
     vbuf[C:C + 16] = jnp.ones((16, LEN), BF16)
 
     for copy in local[3:5]:
         copy.wait()
     local[2].wait()
     temb = mm(feats, wtime[...])
-
-    alone_count = base_mine[0].astype(jnp.int32) + base_mine[1].astype(jnp.int32)
-    pl.semaphore_wait(barrier, 15 + 3 + 7 + 2 - alone_count)
-
-    each(1, 4, lambda k: push(zsrc, yin.at[y], ys, yr, i, 4 * z + lax.rem(y + k, 4)))
 
     emb = left[0:64].astype(F32)
     gain = gain_ref[...]
@@ -268,58 +261,59 @@
             def _():
                 push(basesrc.at[n], basein.at[half], bs.at[n], br.at[half], source_i, base_j[n])
 
-    def attend(lap):
-        packed = latents[lap].reshape(HALF, 128).T
+    chunk = rows_of(pos)
+    low = low_lanes[0:16]
+
+    def project(lap, n):
+        packed = latents[lap, n].T
         zb = jnp.concatenate([packed[0:64], packed[64:128]], axis=1)
         ztr[0:64] = zb
         ztr[128:192] = zb
-
-        def project(n):
-            cols = pl.ds(pl.multiple_of(n * KBLK, KBLK), KBLK)
-            out = mm(wqkv[...], ztr[:, cols])
-            yq, yk, yv, yg = out[0:128], out[128:256], out[256:320], out[320:384]
-            mean_square = (jnp.sum(ztr[0:64, cols].astype(F32) * yg, axis=0, keepdims=True) + t_square) * (1.0 / D)
-            square = jnp.maximum(mean_square, 0.0) + EPS
-            aq = lax.rsqrt(jnp.mean(yq * yq, axis=0, keepdims=True) + EPS * square)
-            ak = lax.rsqrt(jnp.mean(yk * yk, axis=0, keepdims=True) + EPS * square)
-            qbuf[:, cols] = (yq * aq * scale_col).astype(BF16)
-            kbuf[cols, :] = (yk * ak).astype(BF16).T
-            vbuf[0:C, cols] = (yv * lax.rsqrt(square)).astype(BF16)
-
-        loop(0, LEN // KBLK, project)
-
-        def block_of(block):
-            outs = []
-            for side in range(2):
-                q = qbuf[:, pl.ds(pl.multiple_of(side * HALF + block * QBLK, QBLK), QBLK)]
-                acc = jnp.zeros((C + 16, QBLK), F32)
-                for m in range(LEN // KBLK):
-                    weights = jnp.exp2(mm(kbuf[m * KBLK:(m + 1) * KBLK], q))
-                    acc = acc + mm(vbuf[:, m * KBLK:(m + 1) * KBLK], weights.astype(BF16))
-                outs.append(acc[0:C] / acc[C:C + 1])
-            heads[lap, block] = jnp.concatenate(outs, axis=0).astype(BF16).T
-            group(lambda n, ti, tj: push(
-                heads.at[lap, block, rows_of(n), :], red.at[lap, pos, block], us.at[lap], ur.at[lap], ti, tj))
-
-        loop(0, 3, block_of)
-
-    def reduce_heads(lap):
-        chunk = rows_of(pos)
-        red[lap, pos] = heads[lap, :, chunk, :]
-        latent = latents[lap, :, chunk, :].reshape(ROWS, 128)
+        cols = slice(n * KBLK, (n + 1) * KBLK)
+        out = mm(wqkv[...], ztr[...])
+        yq, yk, yv, yg = out[0:128], out[128:256], out[256:320], out[320:384]
+        mean_square = (jnp.sum(zb.astype(F32) * yg, axis=0, keepdims=True) + t_square) * (1.0 / D)
+        square = jnp.maximum(mean_square, 0.0) + EPS
+        aq = lax.rsqrt(jnp.mean(yq * yq, axis=0, keepdims=True) + EPS * square)
+        ak = lax.rsqrt(jnp.mean(yk * yk, axis=0, keepdims=True) + EPS * square)
+        qbuf[:, cols] = (yq * aq * scale_col).astype(BF16)
+        kbuf[cols, :] = (yk * ak).astype(BF16).T
+        vbuf[0:C, cols] = (yv * lax.rsqrt(square)).astype(BF16)
+
+    def attend(block, keys, accs):
+        out = []
+        for side in range(2):
+            q = qbuf[:, block * KBLK + side * QBLK:block * KBLK + (side + 1) * QBLK]
+            acc = accs[side]
+            for m in keys:
+                weights = jnp.exp2(mm(kbuf[m * KBLK:(m + 1) * KBLK], q))
+                part = mm(vbuf[:, m * KBLK:(m + 1) * KBLK], weights.astype(BF16))
+                acc = part if acc is None else acc + part
+            out.append(acc)
+        return out
+
+    def finish(lap, block, accs):
+        outs = [acc[0:C] / acc[C:C + 1] for acc in accs]
+        heads[lap, block] = jnp.concatenate(outs, axis=0).astype(BF16).T
+        group(lambda n, ti, tj: push(
+            heads.at[lap, block, rows_of(n), :], red.at[lap, block, pos], us.at[lap], ur.at[lap, block], ti, tj))
+
+    def reduce_heads(lap, block):
+        red[lap, block, pos] = heads[lap, block, chunk, :]
+        latent = latents[lap, block, chunk, :]
         total = mm(jnp.concatenate([latent, latent, latent], axis=1), cdiag[...]) + crow[0:1]
-        await_bytes(red.at[lap, 0:STEPS - 1], ur.at[lap])
+        await_bytes(red.at[lap, block, 0:STEPS - 1], ur.at[lap, block])
         for h in range(STEPS):
-            total = total + red[lap, h].astype(F32).reshape(ROWS, 128)
-        vsrc[lap] = total.astype(BF16)
-        low = low_lanes[0:16]
-        parts = [total[0:16], total[16:32], total[32:48]]
-        turned = [pltpu.roll(part, C, 1) for part in parts]
-        for side, (first_part, second_part, third_part) in enumerate((
-            (parts[0], turned[1], parts[2]), (turned[0], parts[1], turned[2]),
-        )):
-            vpack[lap, side, 0:16] = jnp.where(low, first_part, second_part).astype(BF16)
-            vpack[lap, side, 16:32] = jnp.where(low, third_part, 0.0).astype(BF16)
+            total = total + red[lap, block, h].astype(F32)
+        return total
+
+    def pack_first(lap, first_part, second_part):
+        vpack[lap, 0, 0:16] = jnp.where(low, first_part, pltpu.roll(second_part, C, 1)).astype(BF16)
+        vpack[lap, 1, 0:16] = jnp.where(low, pltpu.roll(first_part, C, 1), second_part).astype(BF16)
+
+    def pack_last(lap, part):
+        vpack[lap, 0, 16:32] = jnp.where(low, part, 0.0).astype(BF16)
+        vpack[lap, 1, 16:32] = jnp.where(low, pltpu.roll(part, C, 1), 0.0).astype(BF16)
 
     first_i = lax.div(s, 2)
 
@@ -330,92 +324,123 @@
         wanted = to_i >= first_i
         return to_i, to_j, jnp.logical_and(wanted, mine), jnp.logical_and(wanted, jnp.logical_not(mine))
 
-    def to_owners(src, dst, n):
+    def to_owners(src, dst, rows, n):
         def one(k):
             to_i, to_j, here, there = owner_case(k)
 
             @pl.when(here)
             def _():
-                dst[s] = src[k % 2]
+                dst[s, rows] = src[k % 2, rows]
 
             @pl.when(there)
             def _():
-                push(src.at[k % 2], dst.at[s], fs.at[n, k], fr.at[n], to_i, to_j)
+                push(src.at[k % 2, rows], dst.at[s, rows], fs.at[n, k], fr.at[n], to_i, to_j)
         each(0, 16, one)
 
-    def owners_sent(src, n):
+    def owners_sent(src, rows, n):
         def one(k):
             @pl.when(owner_case(k)[3])
             def _():
-                await_bytes(src.at[k % 2], fs.at[n, k])
+                await_bytes(src.at[k % 2, rows], fs.at[n, k])
         each(0, 16, one)
 
     alone = jnp.logical_and(own_chunk == pos, first_i <= i)
 
-    def owner_sums(dst, n):
+    def owner_sums(dst, rows, n):
         for pair in range(COLS):
             for own in range(2):
                 @pl.when(jnp.logical_and(i == pair, alone == (own == 1)))
                 def _():
-                    await_bytes(dst.at[0:2 * pair + 2 - own], fr.at[n])
-        even = jnp.zeros((32, 128), F32)
+                    await_bytes(dst.at[0:2 * pair + 2 - own, rows], fr.at[n])
+        even = jnp.zeros((rows.stop - rows.start, 128), F32)
         odd = even
         for k in range(STEPS):
-            later = delta_ref[k:k + 1] * dst[k].astype(F32)
+            later = delta_ref[k:k + 1] * dst[k, rows].astype(F32)
             even = even + jnp.where(k <= 2 * i, later, 0.0)
             odd = odd + jnp.where(k == 2 * i + 1, later, 0.0)
         return even, even + odd
 
-    chunk = rows_of(pos)
+    all_rows, early_rows, late_rows = slice(0, 32), slice(0, 16), slice(16, 32)
+    blocks = range(3)
+    even_step = lax.rem(s, 2) == 0
+    partner = seq_of(s + 1 - 2 * lax.rem(s, 2), p)
+    delta_low = jnp.sum(jnp.where(step_row == 2 * z, delta, 0.0), axis=0, keepdims=True)
+    delta_high = jnp.sum(jnp.where(step_row == 2 * z + 1, delta, 0.0), axis=0, keepdims=True)
+    velocities = {}
+    lows = {}
+
+    def sum_heads(block):
+        velocities[block] = reduce_heads(0, block)
+        vsrc[block] = velocities[block].astype(BF16)
+        push(vsrc.at[block], mate.at[block], ms.at[block], mr.at[block], i, partner)
+
+    def sum_pair(block):
+        mine = vsrc[block].astype(F32)
+        await_bytes(mate.at[block], mr.at[block])
+        other = mate[block].astype(F32)
+        lows[block] = delta_low * jnp.where(even_step, mine, other)
+        pair = (lows[block] + delta_high * jnp.where(even_step, other, mine)).astype(BF16)
+        gat[block, z] = pair
+        psend[block] = pair
+        each(1, 8, lambda k: push(
+            psend.at[block], gat.at[block, z], gs.at[block], gr.at[block], i, 4 * lax.rem(z + k, 8) + y))
+
+    def next_latent(block):
+        rows = slice(block * 16, (block + 1) * 16)
+        latent = jnp.where(low, basein[0, rows], basein[1, rows]) + jnp.where(even_step, 0.0, lows[block])
+        await_bytes(gat.at[block, 0:7], gr.at[block])
+        for n in range(8):
+            latent = latent + jnp.where(n < z, gat[block, n].astype(F32), 0.0)
+        latent = latent.astype(BF16)
+        zsend[block] = latent
+        latents[1, block, chunk, :] = latent
+        group(lambda n, ti, tj: push(
+            zsend.at[block], latents.at[1, block, chunk, :], ps.at[block], pr.at[block], ti, tj))
+
+    def await_latents(block):
+        await_bytes(latents.at[1, block, 0:15 * 16, :], pr.at[block])
+
     await_bytes(zp.at[:, 0:128, :], cr)
-
-    def iteration(lap):
-        attend(lap)
-
-        @pl.when(lap == 0)
+    for block in blocks:
+        project(0, block)
+    for block in blocks:
+        finish(0, block, attend(block, blocks, (None, None)))
+        if block:
+            sum_heads(block - 1)
+    sum_pair(0)
+    send_base()
+    sum_heads(2)
+    sum_pair(1)
+    for n in range(2):
+        @pl.when(jnp.logical_not(from_mine[n]))
         def _():
-            send_base()
-
-        @pl.when(lap == 1)
-        def _():
-            first_sums[0], first_sums[1] = owner_sums(fin0, 0)
-
-        reduce_heads(lap)
-
-        @pl.when(lap == 0)
-        def _():
-            even = lax.rem(s, 2) == 0
-            partner = seq_of(s + 1 - 2 * lax.rem(s, 2), p)
-            push(vsrc.at[0], mate, ms, mr, i, partner)
-            delta_low = jnp.sum(jnp.where(step_row == 2 * z, delta, 0.0), axis=0, keepdims=True)
-            delta_high = jnp.sum(jnp.where(step_row == 2 * z + 1, delta, 0.0), axis=0, keepdims=True)
-            mine = vsrc[0].astype(F32)
-            await_bytes(mate, mr)
-            other = mate[...].astype(F32)
-            low = delta_low * jnp.where(even, mine, other)
-            pair = (low + delta_high * jnp.where(even, other, mine)).astype(BF16)
-            gat[z] = pair
-            psend[...] = pair
-            each(1, 8, lambda k: push(psend, gat.at[z], gs, gr, i, 4 * lax.rem(z + k, 8) + y))
-            for n in range(2):
-                @pl.when(jnp.logical_not(from_mine[n]))
-                def _():
-                    await_bytes(basein.at[n], br.at[n])
-            latent = jnp.where(low_lanes, basein[0], basein[1]) + jnp.where(even, 0.0, low)
-            await_bytes(gat.at[0:7], gr)
-            for n in range(8):
-                latent = latent + jnp.where(n < z, gat[n].astype(F32), 0.0)
-            latent = latent.reshape(3, 16, 128).astype(BF16)
-            zsend[...] = latent
-            zp2[:, chunk, :] = latent
-            group(lambda n, ti, tj: push(zsend, zp2.at[:, chunk, :], ps, pr, ti, tj))
-            to_owners(vpack.at[0], fin0, 0)
-            await_bytes(zp2.at[:, 0:15 * 16, :], pr)
-
-    loop(0, 2, iteration)
-    to_owners(vpack.at[1], fin1, 1)
-
-    even, odd = owner_sums(fin1, 1)
+            await_bytes(basein.at[n], br.at[n])
+    next_latent(0)
+    sum_pair(2)
+    next_latent(1)
+    pack_first(0, velocities[0], velocities[1])
+    pack_last(0, velocities[2])
+
+    await_latents(0)
+    project(1, 0)
+    next_latent(2)
+    to_owners(vpack.at[0], fin0, all_rows, 0)
+    await_latents(1)
+    project(1, 1)
+    early = [attend(block, (0, 1), (None, None)) for block in (0, 1)]
+    await_latents(2)
+    project(1, 2)
+    for block in (0, 1):
+        finish(1, block, attend(block, (2,), early[block]))
+    finish(1, 2, attend(2, blocks, (None, None)))
+    pack_first(1, reduce_heads(1, 0), reduce_heads(1, 1))
+    to_owners(vpack.at[1], fin1, early_rows, 1)
+    first_sums[0], first_sums[1] = owner_sums(fin0, all_rows, 0)
+    pack_last(1, reduce_heads(1, 2))
+    to_owners(vpack.at[1], fin1, late_rows, 2)
+
+    even, odd = (
+        jnp.concatenate(parts, axis=0) for parts in zip(owner_sums(fin1, early_rows, 1), owner_sums(fin1, late_rows, 2)))
     change_even = even - first_sums[0]
     change_odd = odd - first_sums[1]
 
@@ -446,13 +471,15 @@
 
     await_bytes(ein.at[0:7], es.at[0])
     await_bytes(ein.at[8:11], es.at[1])
-    await_bytes(mate, ms)
-    await_bytes(red.at[0, 0:STEPS - 1], us.at[0])
-    await_bytes(red.at[1, 0:STEPS - 1], us.at[1])
-    await_bytes(gat.at[0:7], gs)
-    await_bytes(zp2.at[:, 0:15 * 16, :], ps)
-    owners_sent(vpack.at[0], 0)
-    owners_sent(vpack.at[1], 1)
+    for lap in range(2):
+        await_bytes(red.at[lap, :, 0:STEPS - 1], us.at[lap])
+    for block in blocks:
+        await_bytes(gat.at[block, 0:7], gs.at[block])
+        await_bytes(latents.at[1, block, 0:15 * 16, :], ps.at[block])
+        await_bytes(mate.at[block], ms.at[block])
+    owners_sent(vpack.at[0], all_rows, 0)
+    owners_sent(vpack.at[1], early_rows, 1)
+    owners_sent(vpack.at[1], late_rows, 2)
     await_bytes(yin.at[0:3], ys)
     await_bytes(nin.at[0:COLS - 1], ns)
     await_bytes(zp.at[:, 0:7 * 16, :], zs)
@@ -503,25 +530,26 @@
             pltpu.VMEM((2, ROWS, 128), F32),
             pltpu.VMEM((2, 3, QBLK, 128), BF16),
             pltpu.VMEM((2, 3, QBLK, 128), BF16),
-            pltpu.VMEM((2, STEPS, 3, 16, 128), BF16),
-            pltpu.VMEM((2, ROWS, 128), BF16),
+            pltpu.VMEM((2, 3, STEPS, 16, 128), BF16),
+            pltpu.VMEM((3, 16, 128), BF16),
             pltpu.VMEM((2, 2, 32, 128), BF16),
-            pltpu.VMEM((ROWS, 128), BF16),
-            pltpu.VMEM((ROWS, 128), BF16),
-            pltpu.VMEM((8, ROWS, 128), BF16),
+            pltpu.VMEM((3, 16, 128), BF16),
+            pltpu.VMEM((3, 16, 128), BF16),
+            pltpu.VMEM((3, 8, 16, 128), BF16),
             pltpu.VMEM((3, 16, 128), BF16),
             pltpu.VMEM((STEPS, 32, 128), BF16),
             pltpu.VMEM((STEPS, 32, 128), BF16),
             pltpu.VMEM((2, 32, 128), F32),
             pltpu.VMEM((2, 2, 128), F32),
             pltpu.VMEM((12, 2, 128), F32),
-            pltpu.VMEM((256, LEN), BF16),
+            pltpu.VMEM((256, KBLK), BF16),
             pltpu.VMEM((LEN, HEAD), BF16),
             pltpu.VMEM((HEAD, LEN), BF16),
             pltpu.VMEM((C + 16, LEN), BF16),
             dma((14,)),
             dma, dma, dma, dma, dma, dma, dma, dma, dma((2,)), dma((2,)),
-            dma((2,)), dma((2,)), dma, dma, dma, dma, dma((2, STEPS)), dma((2,)), dma((2,)), dma((2,)), dma, dma,
+            dma((2,)), dma((2, 3)), dma((3,)), dma((3,)), dma((3,)), dma((3,)), dma((3, STEPS)), dma((3,)), dma((2,)), dma((2,)),
+            dma((3,)), dma((3,)),
         ],
         compiler_params=pltpu.CompilerParams(
             collective_id=0, has_side_effects=True, vmem_limit_bytes=56 * 1024 * 1024),

time: 78.5 us -> 75.7 us (0.964)
  Pallas kernels: 75.6 us -> 72.8 us
    pallas_call x1, Pallas kernels: 75.6 us -> 72.8 us  [per_device(): pl.pallas_call(kernel, out_shape=(pltpu.VMEM((2, ROWS, C), F32), pltpu.SM...]
where the time goes in v2:
time: 75.7 us; the launch traced here: 75.3 us
  Pallas kernels  72.8 us (96%)
  between operations  1.29 us (2%)
  local copies, waits for them, and re-layouts  1.14 us (2%)
    pallas_call x1, Pallas kernels, per_device(): pl.pallas_call(kernel, out_shape=(pltpu.VMEM((2, ROWS, C), F32), pltpu.SM...  72.8 us

profile of v2, /device:TPU:4, one launch (start us, length us, event | category | flops | bytes accessed | tf_op | source)
XLA Modules:
  0.0 75.3 jit_solution(2939106147595730231)
XLA Ops:
  1.3 72.8 %shard_map.140 = (f32[2,48,64]{2,1,0:T(8,128)S(1)}, f32[2]{0:T(128)S(4)}) custom-call(s32[1]{0:T(128)S(6)} %copy.19.ws_ref, f32[48,64]{1,0:T(8,128)} %start_hbm.1, bf16[2,48,64]{2,1,0:T(8,128)(2,1)} %noise_hbm.1, f32[1,3072]{1,0:T(1,128)} %bitcast.5, f32[1,128]{1,0:T(1,128)} %bitcast.6, f32[1,128]{1,0:T(1,128)} %bitcast.7, bf16[64,3072]{1,0:T(8,128)(2,1)} %wembed_hbm.1, ...), custom_call_target="tpu_custom_call" | custom-call | tf_op jit(solution)/shard_map/pallas_call | solution.py:500
  74.1 0.6 copy.17
  74.7 0.5 copy.18

commit v3 on v2

--- a/solution.py
+++ b/solution.py
@@ -51,10 +51,7 @@
 
 def split(x):
     hi = x.astype(BF16)
-    rest = x - hi.astype(F32)
-    mid = rest.astype(BF16)
-    low = (rest - mid.astype(F32)).astype(BF16)
-    return hi, mid, low
+    return hi, (x - hi.astype(F32)).astype(BF16)
 
 
 def mm(a, b):
@@ -70,7 +67,7 @@
     delta_ref, coeff_ref,
     zsrc, yin, slab, nsrc, nin, basesrc, basein,
     latents, heads, red, vsrc, vpack, mate, psend, gat, zsend, fin0, fin1, first_sums, esrc, ein,
-    ztr, kbuf, qbuf, vbuf,
+    ztr, kbuf, qvbuf,
     wsem, ys, yr, zs, zr, cs, cr, ns, nr, bs, br, us, ur, gs, gr, ps, pr, fs, fr, es, er, ms, mr,
 ):
     i = lax.axis_index("step")
@@ -117,7 +114,7 @@
     pairs = [
         (start_hbm, start_ref), (noise_hbm, noise_ref), (wtime_hbm, wtime), (wembed_hbm, left.at[0:64, :]),
         (gain_hbm, gain_ref), (wembed_hbm, right.at[128:192, :]), (wfinal_hbm, right.at[0:64, :]),
-        (wfinal_hbm, right.at[64:128, :]), (wo_hbm.at[pl.ds(head, HEAD), :], left.at[112:240, :]),
+        (wfinal_hbm, right.at[64:128, :]), (wo_hbm.at[pl.ds(head, HEAD), :], left.at[96:224, :]),
         (qg_hbm, qg_ref), (kg_hbm, kg_ref),
     ] + [
         (w.at[:, pl.ds(head, HEAD)], wall.at[:, n * HEAD:(n + 1) * HEAD]) for n, w in enumerate((wq_hbm, wk_hbm, wv_hbm))
@@ -175,7 +172,6 @@
     for n in range(2):
         ztr[128 * n + 64:128 * n + 128] = jnp.where(
             lax.broadcasted_iota(jnp.int32, (64, KBLK), 0) == 0, 1.0, 0.0).astype(BF16)
-    vbuf[C:C + 16] = jnp.ones((16, LEN), BF16)
 
     for copy in local[3:5]:
         copy.wait()
@@ -204,16 +200,16 @@
     for copy in local[5:]:
         copy.wait()
     folded = mm(fold[...], wall[...])
-    folded = folded[0:80] + folded[80:160] + folded[160:240]
+    folded = folded[0:80] + folded[80:160]
     both = lax.dot_general(left[...], right[...], (((1,), (1,)), ((), ())), preferred_element_type=F32)
     cdup = both[0:64, 0:128]
     gram = both[0:64, 128:256]
-    mout = both[112:240, 0:128]
+    mout = both[96:224, 0:128]
     lanes64 = lax.broadcasted_iota(jnp.int32, (64, 128), 1)
     diag = jnp.concatenate([jnp.where(lanes64 < C, cdup, 0.0), jnp.where(lanes64 < C, 0.0, cdup)], axis=0)
     for n, part in enumerate(split(diag)):
         cdiag[n * 128:(n + 1) * 128] = part
-    crow[...] = (both[64:72, 0:128] + both[80:88, 0:128] + both[96:104, 0:128])
+    crow[...] = both[64:72, 0:128] + both[80:88, 0:128]
 
     await_bytes(zp.at[:, 0:7 * 16, :], zr)
     core_rows = pl.ds(pl.multiple_of(128 * c, 128), 128)
@@ -276,32 +272,36 @@
         square = jnp.maximum(mean_square, 0.0) + EPS
         aq = lax.rsqrt(jnp.mean(yq * yq, axis=0, keepdims=True) + EPS * square)
         ak = lax.rsqrt(jnp.mean(yk * yk, axis=0, keepdims=True) + EPS * square)
-        qbuf[:, cols] = (yq * aq * scale_col).astype(BF16)
-        kbuf[cols, :] = (yk * ak).astype(BF16).T
-        vbuf[0:C, cols] = (yv * lax.rsqrt(square)).astype(BF16)
+        kbuf[:, cols] = (yk * ak).astype(BF16)
+        rows = jnp.concatenate([yq * aq * scale_col, yv * lax.rsqrt(square), jnp.ones((C, KBLK), F32)], axis=0)
+        qvbuf[cols, :] = rows.astype(BF16).T
 
     def attend(block, keys, accs):
         out = []
         for side in range(2):
-            q = qbuf[:, block * KBLK + side * QBLK:block * KBLK + (side + 1) * QBLK]
+            q = qvbuf[block * KBLK + side * QBLK:block * KBLK + (side + 1) * QBLK, 0:HEAD]
             acc = accs[side]
             for m in keys:
-                weights = jnp.exp2(mm(kbuf[m * KBLK:(m + 1) * KBLK], q))
-                part = mm(vbuf[:, m * KBLK:(m + 1) * KBLK], weights.astype(BF16))
+                here = slice(m * KBLK, (m + 1) * KBLK)
+                weights = jnp.exp2(mm(q, kbuf[:, here])).astype(BF16)
+                part = mm(weights, qvbuf[here, HEAD:])
                 acc = part if acc is None else acc + part
             out.append(acc)
         return out
 
+    low_block = lax.broadcasted_iota(jnp.int32, (QBLK, 128), 1) < C
+
     def finish(lap, block, accs):
-        outs = [acc[0:C] / acc[C:C + 1] for acc in accs]
-        heads[lap, block] = jnp.concatenate(outs, axis=0).astype(BF16).T
+        first_acc, second_acc = accs
+        heads[lap, block] = jnp.where(
+            low_block, first_acc / pltpu.roll(first_acc, C, 1), pltpu.roll(second_acc, C, 1) / second_acc).astype(BF16)
         group(lambda n, ti, tj: push(
             heads.at[lap, block, rows_of(n), :], red.at[lap, block, pos], us.at[lap], ur.at[lap, block], ti, tj))
 
     def reduce_heads(lap, block):
         red[lap, block, pos] = heads[lap, block, chunk, :]
         latent = latents[lap, block, chunk, :]
-        total = mm(jnp.concatenate([latent, latent, latent], axis=1), cdiag[...]) + crow[0:1]
+        total = mm(jnp.concatenate([latent, latent], axis=1), cdiag[...]) + crow[0:1]
         await_bytes(red.at[lap, block, 0:STEPS - 1], ur.at[lap, block])
         for h in range(STEPS):
             total = total + red[lap, block, h].astype(F32)
@@ -317,34 +317,29 @@
 
     first_i = lax.div(s, 2)
 
-    def owner_case(k):
-        to_i = k // 2
-        to_j = first_block + 2 * (k % 2)
-        mine = jnp.logical_and(to_i == i, to_j == j)
-        wanted = to_i >= first_i
-        return to_i, to_j, jnp.logical_and(wanted, mine), jnp.logical_and(wanted, jnp.logical_not(mine))
+    alone = jnp.logical_and(own_chunk == pos, first_i <= i)
 
     def to_owners(src, dst, rows, n):
+        @pl.when(alone)
+        def _():
+            dst[s, rows] = src[half, rows]
+
         def one(k):
-            to_i, to_j, here, there = owner_case(k)
-
-            @pl.when(here)
+            to_i = k // 2
+            to_j = first_block + 2 * (k % 2)
+            mine = jnp.logical_and(to_i == i, to_j == j)
+
+            @pl.when(jnp.logical_and(to_i >= first_i, jnp.logical_not(mine)))
             def _():
-                dst[s, rows] = src[k % 2, rows]
-
-            @pl.when(there)
-            def _():
-                push(src.at[k % 2, rows], dst.at[s, rows], fs.at[n, k], fr.at[n], to_i, to_j)
+                push(src.at[k % 2, rows], dst.at[s, rows], fs.at[n], fr.at[n], to_i, to_j)
         each(0, 16, one)
 
-    def owners_sent(src, rows, n):
-        def one(k):
-            @pl.when(owner_case(k)[3])
-            def _():
-                await_bytes(src.at[k % 2, rows], fs.at[n, k])
-        each(0, 16, one)
-
-    alone = jnp.logical_and(own_chunk == pos, first_i <= i)
+    def owners_sent(dst, rows, n):
+        for pair in range(COLS):
+            for own in range(2):
+                @pl.when(jnp.logical_and(first_i == pair, alone == (own == 1)))
+                def _():
+                    await_bytes(dst.at[0:2 * (COLS - pair) - own, rows], fs.at[n])
 
     def owner_sums(dst, rows, n):
         for pair in range(COLS):
@@ -456,6 +451,24 @@
     each(1, 8, lambda k: push(esrc.at[0], ein.at[z], es.at[0], er.at[0], i, 4 * lax.rem(z + k, 8) + y))
     for n, total in enumerate((basesrc[1] + unpack(even), basesrc[2] + unpack(odd))):
         out_ref[n] = total[:, 0:C]
+    for lap in range(2):
+        await_bytes(red.at[lap, :, 0:STEPS - 1], us.at[lap])
+    for block in blocks:
+        await_bytes(gat.at[block, 0:7], gs.at[block])
+        await_bytes(latents.at[1, block, 0:15 * 16, :], ps.at[block])
+        await_bytes(mate.at[block], ms.at[block])
+    owners_sent(fin0, all_rows, 0)
+    owners_sent(fin1, early_rows, 1)
+    owners_sent(fin1, late_rows, 2)
+    await_bytes(yin.at[0:3], ys)
+    await_bytes(nin.at[0:COLS - 1], ns)
+    await_bytes(zp.at[:, 0:7 * 16, :], zs)
+    await_bytes(zp.at[:, 0:128, :], cs)
+    for n in range(2):
+        @pl.when(jnp.logical_not(base_mine[n]))
+        def _():
+            await_bytes(basesrc.at[n], bs.at[n])
+
     await_bytes(ein.at[0:7], er.at[0])
     total = ein[0]
     for n in range(1, 8):
@@ -471,23 +484,6 @@
 
     await_bytes(ein.at[0:7], es.at[0])
     await_bytes(ein.at[8:11], es.at[1])
-    for lap in range(2):
-        await_bytes(red.at[lap, :, 0:STEPS - 1], us.at[lap])
-    for block in blocks:
-        await_bytes(gat.at[block, 0:7], gs.at[block])
-        await_bytes(latents.at[1, block, 0:15 * 16, :], ps.at[block])
-        await_bytes(mate.at[block], ms.at[block])
-    owners_sent(vpack.at[0], all_rows, 0)
-    owners_sent(vpack.at[1], early_rows, 1)
-    owners_sent(vpack.at[1], late_rows, 2)
-    await_bytes(yin.at[0:3], ys)
-    await_bytes(nin.at[0:COLS - 1], ns)
-    await_bytes(zp.at[:, 0:7 * 16, :], zs)
-    await_bytes(zp.at[:, 0:128, :], cs)
-    for n in range(2):
-        @pl.when(jnp.logical_not(base_mine[n]))
-        def _():
-            await_bytes(basesrc.at[n], bs.at[n])
 
 
 def per_device(
@@ -513,11 +509,11 @@
             pltpu.VMEM((1, HEAD), F32),
             pltpu.VMEM((256, D), BF16),
             pltpu.VMEM((D, 3 * HEAD), BF16),
-            pltpu.VMEM((240, D), BF16),
-            pltpu.VMEM((240, D), BF16),
+            pltpu.VMEM((160, D), BF16),
+            pltpu.VMEM((224, D), BF16),
             pltpu.VMEM((256, D), BF16),
             pltpu.VMEM((384, 256), BF16),
-            pltpu.VMEM((384, 128), BF16),
+            pltpu.VMEM((256, 128), BF16),
             pltpu.VMEM((8, 128), F32),
             pltpu.VMEM((STEPS, 128), F32),
             pltpu.VMEM((STEPS, 128), F32),
@@ -543,12 +539,11 @@
             pltpu.VMEM((2, 2, 128), F32),
             pltpu.VMEM((12, 2, 128), F32),
             pltpu.VMEM((256, KBLK), BF16),
-            pltpu.VMEM((LEN, HEAD), BF16),
             pltpu.VMEM((HEAD, LEN), BF16),
-            pltpu.VMEM((C + 16, LEN), BF16),
+            pltpu.VMEM((LEN, 2 * HEAD), BF16),
             dma((14,)),
             dma, dma, dma, dma, dma, dma, dma, dma, dma((2,)), dma((2,)),
-            dma((2,)), dma((2, 3)), dma((3,)), dma((3,)), dma((3,)), dma((3,)), dma((3, STEPS)), dma((3,)), dma((2,)), dma((2,)),
+            dma((2,)), dma((2, 3)), dma((3,)), dma((3,)), dma((3,)), dma((3,)), dma((3,)), dma((3,)), dma((2,)), dma((2,)),
             dma((3,)), dma((3,)),
         ],
         compiler_params=pltpu.CompilerParams(

time: 75.7 us -> 76.1 us (level)
  no operation moved by 1% of the time
where the time goes in v3:
time: 76.1 us; the launch traced here: 75.7 us
  Pallas kernels  73.1 us (96%)
  between operations  1.45 us (2%)
  local copies, waits for them, and re-layouts  1.14 us (1%)
    pallas_call x1, Pallas kernels, per_device(): pl.pallas_call(kernel, out_shape=(pltpu.VMEM((2, ROWS, C), F32), pltpu.SM...  73.1 us

profile of v3, /device:TPU:4, one launch (start us, length us, event | category | flops | bytes accessed | tf_op | source)
XLA Modules:
  0.0 75.7 jit_solution(13530800377850495278)
XLA Ops:
  1.3 73.1 %shard_map.140 = (f32[2,48,64]{2,1,0:T(8,128)S(1)}, f32[2]{0:T(128)S(4)}) custom-call(s32[1]{0:T(128)S(6)} %copy.19.ws_ref, f32[48,64]{1,0:T(8,128)} %start_hbm.1, bf16[2,48,64]{2,1,0:T(8,128)(2,1)} %noise_hbm.1, f32[1,3072]{1,0:T(1,128)} %bitcast.5, f32[1,128]{1,0:T(1,128)} %bitcast.6, f32[1,128]{1,0:T(1,128)} %bitcast.7, bf16[64,3072]{1,0:T(8,128)(2,1)} %wembed_hbm.1, ...), custom_call_target="tpu_custom_call" | custom-call | tf_op jit(solution)/shard_map/pallas_call | solution.py:496
  74.4 0.6 copy.17
  75.0 0.5 copy.18

commit v4 on v3

--- a/solution.py
+++ b/solution.py
@@ -65,10 +65,10 @@
     start_ref, noise_ref, gain_ref, qg_ref, kg_ref,
     wtime, wall, fold, left, right, wqkv, cdiag, crow,
     delta_ref, coeff_ref,
-    zsrc, yin, slab, nsrc, nin, basesrc, basein,
-    latents, heads, red, vsrc, vpack, mate, psend, gat, zsend, fin0, fin1, first_sums, esrc, ein,
+    zsrc, yin, nsrc, nin, basesrc, basein,
+    latents, heads, red, vsrc, vpack, gat, zsend, fin0, fin1, first_sums, esrc, ein,
     ztr, kbuf, qvbuf,
-    wsem, ys, yr, zs, zr, cs, cr, ns, nr, bs, br, us, ur, gs, gr, ps, pr, fs, fr, es, er, ms, mr,
+    wsem, ys, yr, cs, cr, ns, nr, bs, br, us, ur, gs, gr, ps, pr, fs, fr, es, er,
 ):
     i = lax.axis_index("step")
     j = lax.axis_index("seq")
@@ -110,6 +110,9 @@
 
     zp = latents.at[0]
 
+    def column(fn):
+        each(1, SEQ, lambda k: fn(lax.rem(j + k, SEQ)))
+
     head = pl.multiple_of(p * HEAD, HEAD)
     pairs = [
         (start_hbm, start_ref), (noise_hbm, noise_ref), (wtime_hbm, wtime), (wembed_hbm, left.at[0:64, :]),
@@ -129,8 +132,7 @@
         pl.semaphore_signal(barrier, inc=1, device_id=(to_i, to_j), device_id_type=MESH)
 
     group(lambda n, ti, tj: greet(ti, tj))
-    each(1, 4, lambda k: greet(i, 4 * z + lax.rem(y + k, 4)))
-    each(1, 8, lambda k: greet(i, 4 * lax.rem(z + k, 8) + y))
+    column(lambda tj: greet(i, tj))
     base_j = [seq_of(2 * i + n, source_p) for n in range(2)]
     base_mine = [jnp.logical_and(source_i == i, tj == j) for tj in base_j]
     from_j = [first_block + 2 * n for n in range(2)]
@@ -144,17 +146,30 @@
     local[0].wait()
     z0 = start_ref[...]
     start_dup = jnp.concatenate([z0, z0], axis=1)
-    zsrc[...] = start_dup.astype(BF16)
-    yin[y] = start_dup.astype(BF16)
+    low = low_lanes[0:16]
+    own_half = lax.div(lax.broadcasted_iota(jnp.int32, (16, 128), 1), C) == half
+    pieces = [start_dup[0:16], start_dup[16:32], start_dup[32:48]]
+    packed_start = jnp.concatenate([
+        jnp.where(own_half, pieces[0], pieces[1]), jnp.where(own_half, pieces[2], 0.0)], axis=0).astype(BF16)
+    zsrc[...] = packed_start
+    sends_start = lax.rem(y, 2) == c
+
+    @pl.when(sends_start)
+    def _():
+        yin[8 * half + z] = packed_start
+
     local[1].wait()
     packed_noise = jnp.concatenate([noise_ref[0], noise_ref[1]], axis=1)
     nsrc[...] = packed_noise
     nin[i] = packed_noise
 
     alone_count = base_mine[0].astype(jnp.int32) + base_mine[1].astype(jnp.int32)
-    pl.semaphore_wait(barrier, 15 + 3 + 7 + 2 - alone_count)
-
-    each(1, 4, lambda k: push(zsrc, yin.at[y], ys, yr, i, 4 * z + lax.rem(y + k, 4)))
+    pl.semaphore_wait(barrier, 15 + 31 + 2 - alone_count)
+
+    @pl.when(sends_start)
+    def _():
+        column(lambda tj: push(zsrc, yin.at[8 * half + z], ys, yr, i, tj))
+
 
     first = ws_ref[0]
     index = (lax.broadcasted_iota(jnp.int32, (STEPS, 128), 0) + first).astype(F32)
@@ -188,19 +203,29 @@
     twice_et = 2.0 * jnp.sum(emb * t_row, axis=1, keepdims=True)
     t_square = jnp.sum(t_row * t_row, axis=1, keepdims=True)
 
-    await_bytes(yin.at[0:3], yr)
-    slab_now = jnp.where(low_lanes, yin[c].astype(F32), yin[c + 2].astype(F32)).reshape(3, 16, 128).astype(BF16)
-    slab[...] = slab_now
-    slab_rows = rows_of(8 * c + z)
-    zp[:, slab_rows, :] = slab_now
-    each(1, 8, lambda k: push(slab, zp.at[:, slab_rows, :], zs, zr, i, 4 * lax.rem(z + k, 8) + y))
-
     each(1, COLS, lambda k: push(nsrc, nin.at[i], ns, nr, lax.rem(i + k, COLS), j))
 
     for copy in local[5:]:
         copy.wait()
     folded = mm(fold[...], wall[...])
     folded = folded[0:80] + folded[80:160]
+    @pl.when(sends_start)
+    def _():
+        await_bytes(yin.at[0:15], yr)
+
+    @pl.when(jnp.logical_not(sends_start))
+    def _():
+        await_bytes(yin, yr)
+
+    for n in range(8):
+        below, above = yin[n].astype(F32), yin[8 + n].astype(F32)
+        there = rows_of(8 * c + n)
+        zp[0, there, :] = jnp.where(low, below[0:16], above[0:16]).astype(BF16)
+        zp[1, there, :] = pltpu.roll(jnp.where(low, above[0:16], below[0:16]), C, 1).astype(BF16)
+        zp[2, there, :] = jnp.where(low, below[16:32], above[16:32]).astype(BF16)
+    core_rows = pl.ds(pl.multiple_of(128 * c, 128), 128)
+    push(zp.at[:, core_rows, :], zp.at[:, core_rows, :], cs, cr, i + 1 - 2 * c, j)
+
     both = lax.dot_general(left[...], right[...], (((1,), (1,)), ((), ())), preferred_element_type=F32)
     cdup = both[0:64, 0:128]
     gram = both[0:64, 128:256]
@@ -210,10 +235,6 @@
     for n, part in enumerate(split(diag)):
         cdiag[n * 128:(n + 1) * 128] = part
     crow[...] = both[64:72, 0:128] + both[80:88, 0:128]
-
-    await_bytes(zp.at[:, 0:7 * 16, :], zr)
-    core_rows = pl.ds(pl.multiple_of(128 * c, 128), 128)
-    push(zp.at[:, core_rows, :], zp.at[:, core_rows, :], cs, cr, i + 1 - 2 * c, j)
 
     value_fold = jnp.dot(folded[:, 256:384], mout, precision=lax.Precision.HIGHEST, preferred_element_type=F32)
     wide = jnp.concatenate([folded[:, 0:256], value_fold], axis=1)
@@ -357,35 +378,24 @@
 
     all_rows, early_rows, late_rows = slice(0, 32), slice(0, 16), slice(16, 32)
     blocks = range(3)
-    even_step = lax.rem(s, 2) == 0
-    partner = seq_of(s + 1 - 2 * lax.rem(s, 2), p)
-    delta_low = jnp.sum(jnp.where(step_row == 2 * z, delta, 0.0), axis=0, keepdims=True)
-    delta_high = jnp.sum(jnp.where(step_row == 2 * z + 1, delta, 0.0), axis=0, keepdims=True)
     velocities = {}
-    lows = {}
 
     def sum_heads(block):
         velocities[block] = reduce_heads(0, block)
         vsrc[block] = velocities[block].astype(BF16)
-        push(vsrc.at[block], mate.at[block], ms.at[block], mr.at[block], i, partner)
-
-    def sum_pair(block):
-        mine = vsrc[block].astype(F32)
-        await_bytes(mate.at[block], mr.at[block])
-        other = mate[block].astype(F32)
-        lows[block] = delta_low * jnp.where(even_step, mine, other)
-        pair = (lows[block] + delta_high * jnp.where(even_step, other, mine)).astype(BF16)
-        gat[block, z] = pair
-        psend[block] = pair
-        each(1, 8, lambda k: push(
-            psend.at[block], gat.at[block, z], gs.at[block], gr.at[block], i, 4 * lax.rem(z + k, 8) + y))
+        gat[block, s] = velocities[block].astype(BF16)
+
+        def send(k):
+            to = lax.rem(s + k, STEPS)
+            push(vsrc.at[block], gat.at[block, s], gs.at[block], gr.at[block], i, seq_of(to, p))
+        each(1, STEPS, send)
 
     def next_latent(block):
         rows = slice(block * 16, (block + 1) * 16)
-        latent = jnp.where(low, basein[0, rows], basein[1, rows]) + jnp.where(even_step, 0.0, lows[block])
-        await_bytes(gat.at[block, 0:7], gr.at[block])
-        for n in range(8):
-            latent = latent + jnp.where(n < z, gat[block, n].astype(F32), 0.0)
+        latent = jnp.where(low, basein[0, rows], basein[1, rows])
+        await_bytes(gat.at[block, 0:STEPS - 1], gr.at[block])
+        for n in range(STEPS):
+            latent = latent + jnp.where(n < s, delta_ref[n:n + 1] * gat[block, n].astype(F32), 0.0)
         latent = latent.astype(BF16)
         zsend[block] = latent
         latents[1, block, chunk, :] = latent
@@ -402,16 +412,13 @@
         finish(0, block, attend(block, blocks, (None, None)))
         if block:
             sum_heads(block - 1)
-    sum_pair(0)
     send_base()
     sum_heads(2)
-    sum_pair(1)
     for n in range(2):
         @pl.when(jnp.logical_not(from_mine[n]))
         def _():
             await_bytes(basein.at[n], br.at[n])
     next_latent(0)
-    sum_pair(2)
     next_latent(1)
     pack_first(0, velocities[0], velocities[1])
     pack_last(0, velocities[2])
@@ -446,44 +453,39 @@
     sum_even = jnp.sum(change_even * change_even, axis=0, keepdims=True)
     sum_odd = jnp.sum(change_odd * change_odd, axis=0, keepdims=True)
     partial = jnp.where(row == 0, sum_even, sum_odd)
-    esrc[0] = partial
-    ein[z] = partial
-    each(1, 8, lambda k: push(esrc.at[0], ein.at[z], es.at[0], er.at[0], i, 4 * lax.rem(z + k, 8) + y))
+    esrc[...] = partial
+    ein[j] = partial
+    column(lambda tj: push(esrc, ein.at[j], es, er, i, tj))
     for n, total in enumerate((basesrc[1] + unpack(even), basesrc[2] + unpack(odd))):
         out_ref[n] = total[:, 0:C]
     for lap in range(2):
         await_bytes(red.at[lap, :, 0:STEPS - 1], us.at[lap])
     for block in blocks:
-        await_bytes(gat.at[block, 0:7], gs.at[block])
+        await_bytes(gat.at[block, 0:STEPS - 1], gs.at[block])
         await_bytes(latents.at[1, block, 0:15 * 16, :], ps.at[block])
-        await_bytes(mate.at[block], ms.at[block])
     owners_sent(fin0, all_rows, 0)
     owners_sent(fin1, early_rows, 1)
     owners_sent(fin1, late_rows, 2)
-    await_bytes(yin.at[0:3], ys)
+    @pl.when(sends_start)
+    def _():
+        await_bytes(wall.at[0:31 * 32, 0:128], ys)
+
     await_bytes(nin.at[0:COLS - 1], ns)
-    await_bytes(zp.at[:, 0:7 * 16, :], zs)
     await_bytes(zp.at[:, 0:128, :], cs)
     for n in range(2):
         @pl.when(jnp.logical_not(base_mine[n]))
         def _():
             await_bytes(basesrc.at[n], bs.at[n])
 
-    await_bytes(ein.at[0:7], er.at[0])
+    await_bytes(ein.at[0:SEQ - 1], er)
     total = ein[0]
-    for n in range(1, 8):
+    for n in range(1, SEQ):
         total = total + ein[n]
-    esrc[1] = total
-    ein[8 + y] = total
-    each(1, 4, lambda k: push(esrc.at[1], ein.at[8 + y], es.at[1], er.at[1], i, 4 * z + lax.rem(y + k, 4)))
-    await_bytes(ein.at[8:11], er.at[1])
-    total = (ein[8] + ein[9]) + (ein[10] + ein[11])
     total = total * (1.0 / (LEN * C))
     err_ref[0] = jnp.sum(total[0:1] / (coeff_even * coeff_even))
     err_ref[1] = jnp.sum(total[1:2] / (coeff_odd * coeff_odd))
 
-    await_bytes(ein.at[0:7], es.at[0])
-    await_bytes(ein.at[8:11], es.at[1])
+    await_bytes(ein.at[0:SEQ - 1], es)
 
 
 def per_device(
@@ -517,9 +519,8 @@
             pltpu.VMEM((8, 128), F32),
             pltpu.VMEM((STEPS, 128), F32),
             pltpu.VMEM((STEPS, 128), F32),
-            pltpu.VMEM((ROWS, 128), BF16),
-            pltpu.VMEM((4, ROWS, 128), BF16),
-            pltpu.VMEM((3, 16, 128), BF16),
+            pltpu.VMEM((32, 128), BF16),
+            pltpu.VMEM((16, 32, 128), BF16),
             pltpu.VMEM((ROWS, 128), BF16),
             pltpu.VMEM((COLS, ROWS, 128), BF16),
             pltpu.VMEM((3, ROWS, 128), F32),
@@ -529,22 +530,19 @@
             pltpu.VMEM((2, 3, STEPS, 16, 128), BF16),
             pltpu.VMEM((3, 16, 128), BF16),
             pltpu.VMEM((2, 2, 32, 128), BF16),
-            pltpu.VMEM((3, 16, 128), BF16),
-            pltpu.VMEM((3, 16, 128), BF16),
-            pltpu.VMEM((3, 8, 16, 128), BF16),
+            pltpu.VMEM((3, STEPS, 16, 128), BF16),
             pltpu.VMEM((3, 16, 128), BF16),
             pltpu.VMEM((STEPS, 32, 128), BF16),
             pltpu.VMEM((STEPS, 32, 128), BF16),
             pltpu.VMEM((2, 32, 128), F32),
-            pltpu.VMEM((2, 2, 128), F32),
-            pltpu.VMEM((12, 2, 128), F32),
+            pltpu.VMEM((2, 128), F32),
+            pltpu.VMEM((SEQ, 2, 128), F32),
             pltpu.VMEM((256, KBLK), BF16),
             pltpu.VMEM((HEAD, LEN), BF16),
             pltpu.VMEM((LEN, 2 * HEAD), BF16),
             dma((14,)),
-            dma, dma, dma, dma, dma, dma, dma, dma, dma((2,)), dma((2,)),
-            dma((2,)), dma((2, 3)), dma((3,)), dma((3,)), dma((3,)), dma((3,)), dma((3,)), dma((3,)), dma((2,)), dma((2,)),
-            dma((3,)), dma((3,)),
+            dma, dma, dma, dma, dma, dma, dma((2,)), dma((2,)),
+            dma((2,)), dma((2, 3)), dma((3,)), dma((3,)), dma((3,)), dma((3,)), dma((3,)), dma((3,)), dma, dma,
         ],
         compiler_params=pltpu.CompilerParams(
             collective_id=0, has_side_effects=True, vmem_limit_bytes=56 * 1024 * 1024),

time: 76.1 us -> 74.8 us (0.983)
  Pallas kernels: 73.1 us -> 71.8 us
    pallas_call x1, Pallas kernels: 73.1 us -> 71.8 us  [per_device(): pl.pallas_call(kernel, out_shape=(pltpu.VMEM((2, ROWS, C), F32), pltpu.SM...]
where the time goes in v4:
time: 74.8 us; the launch traced here: 74.4 us
  Pallas kernels  71.8 us (96%)
  between operations  1.45 us (2%)
  local copies, waits for them, and re-layouts  1.14 us (2%)
    pallas_call x1, Pallas kernels, per_device(): pl.pallas_call(kernel, out_shape=(pltpu.VMEM((2, ROWS, C), F32), pltpu.SM...  71.8 us

profile of v4, /device:TPU:4, one launch (start us, length us, event | category | flops | bytes accessed | tf_op | source)
XLA Modules:
  0.0 74.4 jit_solution(16123339077854253251)
XLA Ops:
  1.3 71.8 %shard_map.140 = (f32[2,48,64]{2,1,0:T(8,128)S(1)}, f32[2]{0:T(128)S(4)}) custom-call(s32[1]{0:T(128)S(6)} %copy.19.ws_ref, f32[48,64]{1,0:T(8,128)} %start_hbm.1, bf16[2,48,64]{2,1,0:T(8,128)(2,1)} %noise_hbm.1, f32[1,3072]{1,0:T(1,128)} %bitcast.5, f32[1,128]{1,0:T(1,128)} %bitcast.6, f32[1,128]{1,0:T(1,128)} %bitcast.7, bf16[64,3072]{1,0:T(8,128)(2,1)} %wembed_hbm.1, ...), custom_call_target="tpu_custom_call" | custom-call | tf_op jit(solution)/shard_map/pallas_call | solution.py:498
  73.1 0.6 copy.17
  73.7 0.5 copy.18

commit v5 on v4

--- a/solution.py
+++ b/solution.py
@@ -297,23 +297,18 @@
         rows = jnp.concatenate([yq * aq * scale_col, yv * lax.rsqrt(square), jnp.ones((C, KBLK), F32)], axis=0)
         qvbuf[cols, :] = rows.astype(BF16).T
 
-    def attend(block, keys, accs):
-        out = []
-        for side in range(2):
-            q = qvbuf[block * KBLK + side * QBLK:block * KBLK + (side + 1) * QBLK, 0:HEAD]
-            acc = accs[side]
-            for m in keys:
-                here = slice(m * KBLK, (m + 1) * KBLK)
-                weights = jnp.exp2(mm(q, kbuf[:, here])).astype(BF16)
-                part = mm(weights, qvbuf[here, HEAD:])
-                acc = part if acc is None else acc + part
-            out.append(acc)
-        return out
+    def attend(block, side, keys, acc=None):
+        q = qvbuf[block * KBLK + side * QBLK:block * KBLK + (side + 1) * QBLK, 0:HEAD]
+        for m in keys:
+            here = slice(m * KBLK, (m + 1) * KBLK)
+            weights = jnp.exp2(mm(q, kbuf[:, here])).astype(BF16)
+            part = mm(weights, qvbuf[here, HEAD:])
+            acc = part if acc is None else acc + part
+        return acc
 
     low_block = lax.broadcasted_iota(jnp.int32, (QBLK, 128), 1) < C
 
-    def finish(lap, block, accs):
-        first_acc, second_acc = accs
+    def finish(lap, block, first_acc, second_acc):
         heads[lap, block] = jnp.where(
             low_block, first_acc / pltpu.roll(first_acc, C, 1), pltpu.roll(second_acc, C, 1) / second_acc).astype(BF16)
         group(lambda n, ti, tj: push(
@@ -408,35 +403,42 @@
     await_bytes(zp.at[:, 0:128, :], cr)
     for block in blocks:
         project(0, block)
-    for block in blocks:
-        finish(0, block, attend(block, blocks, (None, None)))
-        if block:
-            sum_heads(block - 1)
+    finish(0, 0, attend(0, 0, blocks), attend(0, 1, blocks))
     send_base()
-    sum_heads(2)
+    finish(0, 1, attend(1, 0, blocks), attend(1, 1, blocks))
+    sum_heads(0)
+    first_acc = attend(2, 0, blocks)
+    sum_heads(1)
     for n in range(2):
         @pl.when(jnp.logical_not(from_mine[n]))
         def _():
             await_bytes(basein.at[n], br.at[n])
     next_latent(0)
+    finish(0, 2, first_acc, attend(2, 1, blocks))
     next_latent(1)
     pack_first(0, velocities[0], velocities[1])
-    pack_last(0, velocities[2])
 
     await_latents(0)
     project(1, 0)
-    next_latent(2)
-    to_owners(vpack.at[0], fin0, all_rows, 0)
+    early = {(0, 0): attend(0, 0, (0,))}
+    sum_heads(2)
+    pack_last(0, velocities[2])
+    early[0, 1] = attend(0, 1, (0,))
     await_latents(1)
     project(1, 1)
-    early = [attend(block, (0, 1), (None, None)) for block in (0, 1)]
+    next_latent(2)
+    for side in range(2):
+        early[0, side] = attend(0, side, (1,), early[0, side])
+        early[1, side] = attend(1, side, (0, 1))
+    to_owners(vpack.at[0], fin0, all_rows, 0)
     await_latents(2)
     project(1, 2)
     for block in (0, 1):
-        finish(1, block, attend(block, (2,), early[block]))
-    finish(1, 2, attend(2, blocks, (None, None)))
+        finish(1, block, *(attend(block, side, (2,), early[block, side]) for side in range(2)))
+    first_acc = attend(2, 0, blocks)
     pack_first(1, reduce_heads(1, 0), reduce_heads(1, 1))
     to_owners(vpack.at[1], fin1, early_rows, 1)
+    finish(1, 2, first_acc, attend(2, 1, blocks))
     first_sums[0], first_sums[1] = owner_sums(fin0, all_rows, 0)
     pack_last(1, reduce_heads(1, 2))
     to_owners(vpack.at[1], fin1, late_rows, 2)

time: 74.8 us -> 75.8 us (1.013)
  Pallas kernels: 71.8 us -> 72.8 us
    pallas_call x1, Pallas kernels: 71.8 us -> 72.8 us  [per_device(): pl.pallas_call(kernel, out_shape=(pltpu.VMEM((2, ROWS, C), F32), pltpu.SM...]
where the time goes in v5:
time: 75.8 us; the launch traced here: 75.4 us
  Pallas kernels  72.8 us (96%)
  between operations  1.45 us (2%)
  local copies, waits for them, and re-layouts  1.14 us (2%)
    pallas_call x1, Pallas kernels, per_device(): pl.pallas_call(kernel, out_shape=(pltpu.VMEM((2, ROWS, C), F32), pltpu.SM...  72.8 us

profile of v5, /device:TPU:4, one launch (start us, length us, event | category | flops | bytes accessed | tf_op | source)
XLA Modules:
  0.0 75.4 jit_solution(15715017917814347109)
XLA Ops:
  1.3 72.8 %shard_map.140 = (f32[2,48,64]{2,1,0:T(8,128)S(1)}, f32[2]{0:T(128)S(4)}) custom-call(s32[1]{0:T(128)S(6)} %copy.19.ws_ref, f32[48,64]{1,0:T(8,128)} %start_hbm.1, bf16[2,48,64]{2,1,0:T(8,128)(2,1)} %noise_hbm.1, f32[1,3072]{1,0:T(1,128)} %bitcast.5, f32[1,128]{1,0:T(1,128)} %bitcast.6, f32[1,128]{1,0:T(1,128)} %bitcast.7, bf16[64,3072]{1,0:T(8,128)(2,1)} %wembed_hbm.1, ...), custom_call_target="tpu_custom_call" | custom-call | tf_op jit(solution)/shard_map/pallas_call | solution.py:500
  74.1 0.6 copy.17
  74.7 0.5 copy.18

commit v6 on v4

--- a/solution.py
+++ b/solution.py
@@ -67,7 +67,7 @@
     delta_ref, coeff_ref,
     zsrc, yin, nsrc, nin, basesrc, basein,
     latents, heads, red, vsrc, vpack, gat, zsend, fin0, fin1, first_sums, esrc, ein,
-    ztr, kbuf, qvbuf,
+    ztr, kbuf, qbuf, vbuf,
     wsem, ys, yr, cs, cr, ns, nr, bs, br, us, ur, gs, gr, ps, pr, fs, fr, es, er,
 ):
     i = lax.axis_index("step")
@@ -106,12 +106,31 @@
         def one(k):
             n = lax.rem(pos + k, STEPS)
             fn(n, chunk_i(n), seq_of(s, chunk_p(n)))
-        each(1, STEPS, one)
+        for k in sorted(range(1, STEPS), key=lambda k: -min(k % 4, -k % 4)):
+            one(k)
 
     zp = latents.at[0]
 
     def column(fn):
-        each(1, SEQ, lambda k: fn(lax.rem(j + k, SEQ)))
+        for k in sorted(range(1, SEQ), key=lambda k: abs(k - SEQ // 2)):
+            fn(lax.rem(j + k, SEQ))
+
+    barrier = pltpu.get_barrier_semaphore()
+
+    def greet(to_i, to_j):
+        pl.semaphore_signal(barrier, inc=1, device_id=(to_i, to_j), device_id_type=MESH)
+
+    group(lambda n, ti, tj: greet(ti, tj))
+    column(lambda tj: greet(i, tj))
+    base_j = [seq_of(2 * i + n, source_p) for n in range(2)]
+    base_mine = [jnp.logical_and(source_i == i, tj == j) for tj in base_j]
+    from_j = [first_block + 2 * n for n in range(2)]
+    from_i = lax.div(s, 2)
+    from_mine = [jnp.logical_and(from_i == i, tj == j) for tj in from_j]
+    for n in range(2):
+        @pl.when(jnp.logical_not(from_mine[n]))
+        def _():
+            greet(from_i, from_j[n])
 
     head = pl.multiple_of(p * HEAD, HEAD)
     pairs = [
@@ -125,23 +144,6 @@
     local = [pltpu.make_async_copy(src, dst, wsem.at[n]) for n, (src, dst) in enumerate(pairs)]
     for copy in local:
         copy.start()
-
-    barrier = pltpu.get_barrier_semaphore()
-
-    def greet(to_i, to_j):
-        pl.semaphore_signal(barrier, inc=1, device_id=(to_i, to_j), device_id_type=MESH)
-
-    group(lambda n, ti, tj: greet(ti, tj))
-    column(lambda tj: greet(i, tj))
-    base_j = [seq_of(2 * i + n, source_p) for n in range(2)]
-    base_mine = [jnp.logical_and(source_i == i, tj == j) for tj in base_j]
-    from_j = [first_block + 2 * n for n in range(2)]
-    from_i = lax.div(s, 2)
-    from_mine = [jnp.logical_and(from_i == i, tj == j) for tj in from_j]
-    for n in range(2):
-        @pl.when(jnp.logical_not(from_mine[n]))
-        def _():
-            greet(from_i, from_j[n])
 
     local[0].wait()
     z0 = start_ref[...]
@@ -184,6 +186,7 @@
     feats = jnp.concatenate([jnp.cos(angle), jnp.sin(angle)], axis=1)
     feats = (feats / (1.0 + jnp.exp(-feats))).astype(BF16)
     right[192:256] = jnp.zeros((64, D), BF16)
+    vbuf[C:C + 16] = jnp.ones((16, LEN), BF16)
     for n in range(2):
         ztr[128 * n + 64:128 * n + 128] = jnp.where(
             lax.broadcasted_iota(jnp.int32, (64, KBLK), 0) == 0, 1.0, 0.0).astype(BF16)
@@ -293,29 +296,26 @@
         square = jnp.maximum(mean_square, 0.0) + EPS
         aq = lax.rsqrt(jnp.mean(yq * yq, axis=0, keepdims=True) + EPS * square)
         ak = lax.rsqrt(jnp.mean(yk * yk, axis=0, keepdims=True) + EPS * square)
-        kbuf[:, cols] = (yk * ak).astype(BF16)
-        rows = jnp.concatenate([yq * aq * scale_col, yv * lax.rsqrt(square), jnp.ones((C, KBLK), F32)], axis=0)
-        qvbuf[cols, :] = rows.astype(BF16).T
+        qbuf[:, cols] = (yq * aq * scale_col).astype(BF16)
+        kbuf[cols, :] = (yk * ak).astype(BF16).T
+        vbuf[0:C, cols] = (yv * lax.rsqrt(square)).astype(BF16)
 
     def attend(block, keys, accs):
         out = []
         for side in range(2):
-            q = qvbuf[block * KBLK + side * QBLK:block * KBLK + (side + 1) * QBLK, 0:HEAD]
+            q = qbuf[:, block * KBLK + side * QBLK:block * KBLK + (side + 1) * QBLK]
             acc = accs[side]
             for m in keys:
                 here = slice(m * KBLK, (m + 1) * KBLK)
-                weights = jnp.exp2(mm(q, kbuf[:, here])).astype(BF16)
-                part = mm(weights, qvbuf[here, HEAD:])
+                weights = jnp.exp2(mm(kbuf[here], q)).astype(BF16)
+                part = mm(vbuf[:, here], weights)
                 acc = part if acc is None else acc + part
             out.append(acc)
         return out
 
-    low_block = lax.broadcasted_iota(jnp.int32, (QBLK, 128), 1) < C
-
     def finish(lap, block, accs):
-        first_acc, second_acc = accs
-        heads[lap, block] = jnp.where(
-            low_block, first_acc / pltpu.roll(first_acc, C, 1), pltpu.roll(second_acc, C, 1) / second_acc).astype(BF16)
+        outs = [acc[0:C] / acc[C:C + 1] for acc in accs]
+        heads[lap, block] = jnp.concatenate(outs, axis=0).astype(BF16).T
         group(lambda n, ti, tj: push(
             heads.at[lap, block, rows_of(n), :], red.at[lap, block, pos], us.at[lap], ur.at[lap, block], ti, tj))
 
@@ -388,7 +388,8 @@
         def send(k):
             to = lax.rem(s + k, STEPS)
             push(vsrc.at[block], gat.at[block, s], gs.at[block], gr.at[block], i, seq_of(to, p))
-        each(1, STEPS, send)
+        for k in sorted(range(1, STEPS), key=lambda k: abs(k - STEPS // 2)):
+            send(k)
 
     def next_latent(block):
         rows = slice(block * 16, (block + 1) * 16)
@@ -538,8 +539,9 @@
             pltpu.VMEM((2, 128), F32),
             pltpu.VMEM((SEQ, 2, 128), F32),
             pltpu.VMEM((256, KBLK), BF16),
+            pltpu.VMEM((LEN, HEAD), BF16),
             pltpu.VMEM((HEAD, LEN), BF16),
-            pltpu.VMEM((LEN, 2 * HEAD), BF16),
+            pltpu.VMEM((C + 16, LEN), BF16),
             dma((14,)),
             dma, dma, dma, dma, dma, dma, dma((2,)), dma((2,)),
             dma((2,)), dma((2, 3)), dma((3,)), dma((3,)), dma((3,)), dma((3,)), dma((3,)), dma((3,)), dma, dma,

time: 74.8 us -> 73.2 us (0.979)
  Pallas kernels: 71.8 us -> 70.3 us
    pallas_call x1, Pallas kernels: 71.8 us -> 70.3 us  [per_device(): pl.pallas_call(kernel, out_shape=(pltpu.VMEM((2, ROWS, C), F32), pltpu.SM...]
where the time goes in v6:
time: 73.2 us; the launch traced here: 72.8 us
  Pallas kernels  70.3 us (96%)
  between operations  1.29 us (2%)
  local copies, waits for them, and re-layouts  1.14 us (2%)
    pallas_call x1, Pallas kernels, per_device(): pl.pallas_call(kernel, out_shape=(pltpu.VMEM((2, ROWS, C), F32), pltpu.SM...  70.3 us

profile of v6, /device:TPU:4, one launch (start us, length us, event | category | flops | bytes accessed | tf_op | source)
XLA Modules:
  0.0 72.8 jit_solution(17916915313477052539)
XLA Ops:
  1.3 70.3 %shard_map.140 = (f32[2,48,64]{2,1,0:T(8,128)S(1)}, f32[2]{0:T(128)S(4)}) custom-call(s32[1]{0:T(128)S(6)} %copy.19.ws_ref, f32[48,64]{1,0:T(8,128)} %start_hbm.1, bf16[2,48,64]{2,1,0:T(8,128)(2,1)} %noise_hbm.1, f32[1,3072]{1,0:T(1,128)} %bitcast.5, f32[1,128]{1,0:T(1,128)} %bitcast.6, f32[1,128]{1,0:T(1,128)} %bitcast.7, bf16[64,3072]{1,0:T(8,128)(2,1)} %wembed_hbm.1, ...), custom_call_target="tpu_custom_call" | custom-call | tf_op jit(solution)/shard_map/pallas_call | solution.py:499
  71.6 0.6 copy.17
  72.2 0.5 copy.18

commit v7 on v6

--- a/solution.py
+++ b/solution.py
@@ -301,17 +301,11 @@
         vbuf[0:C, cols] = (yv * lax.rsqrt(square)).astype(BF16)
 
     def attend(block, keys, accs):
-        out = []
-        for side in range(2):
-            q = qbuf[:, block * KBLK + side * QBLK:block * KBLK + (side + 1) * QBLK]
-            acc = accs[side]
-            for m in keys:
-                here = slice(m * KBLK, (m + 1) * KBLK)
-                weights = jnp.exp2(mm(kbuf[here], q)).astype(BF16)
-                part = mm(vbuf[:, here], weights)
-                acc = part if acc is None else acc + part
-            out.append(acc)
-        return out
+        here = slice(keys[0] * KBLK, (keys[-1] + 1) * KBLK)
+        scores = [
+            mm(kbuf[here], qbuf[:, block * KBLK + side * QBLK:block * KBLK + (side + 1) * QBLK]) for side in range(2)]
+        parts = [mm(vbuf[:, here], jnp.exp2(score).astype(BF16)) for score in scores]
+        return [part if acc is None else acc + part for part, acc in zip(parts, accs)]
 
     def finish(lap, block, accs):
         outs = [acc[0:C] / acc[C:C + 1] for acc in accs]

time: 73.2 us -> 73 us (level)
  no operation moved by 1% of the time
where the time goes in v7:
time: 73 us; the launch traced here: 72.8 us
  Pallas kernels  70.4 us (96%)
  between operations  1.29 us (2%)
  local copies, waits for them, and re-layouts  1.14 us (2%)
    pallas_call x1, Pallas kernels, per_device(): pl.pallas_call(kernel, out_shape=(pltpu.VMEM((2, ROWS, C), F32), pltpu.SM...  70.4 us

profile of v7, /device:TPU:4, one launch (start us, length us, event | category | flops | bytes accessed | tf_op | source)
XLA Modules:
  0.0 72.8 jit_solution(9623370112804005087)
XLA Ops:
  1.3 70.4 %shard_map.140 = (f32[2,48,64]{2,1,0:T(8,128)S(1)}, f32[2]{0:T(128)S(4)}) custom-call(s32[1]{0:T(128)S(6)} %copy.19.ws_ref, f32[48,64]{1,0:T(8,128)} %start_hbm.1, bf16[2,48,64]{2,1,0:T(8,128)(2,1)} %noise_hbm.1, f32[1,3072]{1,0:T(1,128)} %bitcast.5, f32[1,128]{1,0:T(1,128)} %bitcast.6, f32[1,128]{1,0:T(1,128)} %bitcast.7, bf16[64,3072]{1,0:T(8,128)(2,1)} %wembed_hbm.1, ...), custom_call_target="tpu_custom_call" | custom-call | tf_op jit(solution)/shard_map/pallas_call | solution.py:493
  71.7 0.6 copy.17
  72.3 0.5 copy.18

commit v8 on v7

--- a/solution.py
+++ b/solution.py
@@ -26,6 +26,8 @@
 COLS = 8
 QBLK = 256
 KBLK = 512
+PARTS = 4
+DBLK = D // PARTS
 
 
 def sigma_of(index):
@@ -133,14 +135,17 @@
             greet(from_i, from_j[n])
 
     head = pl.multiple_of(p * HEAD, HEAD)
-    pairs = [
-        (start_hbm, start_ref), (noise_hbm, noise_ref), (wtime_hbm, wtime), (wembed_hbm, left.at[0:64, :]),
-        (gain_hbm, gain_ref), (wembed_hbm, right.at[128:192, :]), (wfinal_hbm, right.at[0:64, :]),
-        (wfinal_hbm, right.at[64:128, :]), (wo_hbm.at[pl.ds(head, HEAD), :], left.at[96:224, :]),
-        (qg_hbm, qg_ref), (kg_hbm, kg_ref),
-    ] + [
-        (w.at[:, pl.ds(head, HEAD)], wall.at[:, n * HEAD:(n + 1) * HEAD]) for n, w in enumerate((wq_hbm, wk_hbm, wv_hbm))
-    ]
+    widths = [slice(n * DBLK, (n + 1) * DBLK) for n in range(PARTS)]
+    pairs = [(start_hbm, start_ref), (noise_hbm, noise_ref), (gain_hbm, gain_ref), (qg_hbm, qg_ref), (kg_hbm, kg_ref)]
+    for part in widths:
+        pairs += [(wtime_hbm.at[:, part], wtime.at[:, part]), (wembed_hbm.at[:, part], left.at[0:64, part])]
+        pairs += [
+            (w.at[part, pl.ds(head, HEAD)], wall.at[part, n * HEAD:(n + 1) * HEAD]) for n, w in enumerate((wq_hbm, wk_hbm, wv_hbm))
+        ]
+        pairs += [
+            (wfinal_hbm.at[:, part], right.at[0:64, part]),
+            (wo_hbm.at[pl.ds(head, HEAD), part], left.at[96:224, part]),
+        ]
     local = [pltpu.make_async_copy(src, dst, wsem.at[n]) for n, (src, dst) in enumerate(pairs)]
     for copy in local:
         copy.start()
@@ -191,27 +196,40 @@
         ztr[128 * n + 64:128 * n + 128] = jnp.where(
             lax.broadcasted_iota(jnp.int32, (64, KBLK), 0) == 0, 1.0, 0.0).astype(BF16)
 
-    for copy in local[3:5]:
+    each(1, COLS, lambda k: push(nsrc, nin.at[i], ns, nr, lax.rem(i + k, COLS), j))
+
+    for copy in local[2:5]:
         copy.wait()
-    local[2].wait()
-    temb = mm(feats, wtime[...])
-
-    emb = left[0:64].astype(F32)
-    gain = gain_ref[...]
-    for n, part in enumerate(split(jnp.concatenate([emb * gain, temb * gain], axis=0))):
-        fold[n * 80:(n + 1) * 80] = part
-    for n, part in enumerate(split(temb)):
-        left[64 + 16 * n:80 + 16 * n] = part
-    t_row = temb[0:1]
-    twice_et = 2.0 * jnp.sum(emb * t_row, axis=1, keepdims=True)
-    t_square = jnp.sum(t_row * t_row, axis=1, keepdims=True)
-
-    each(1, COLS, lambda k: push(nsrc, nin.at[i], ns, nr, lax.rem(i + k, COLS), j))
-
-    for copy in local[5:]:
-        copy.wait()
-    folded = mm(fold[...], wall[...])
-    folded = folded[0:80] + folded[80:160]
+    sums = [0.0] * 4
+
+    def fold_part(n):
+        part = widths[n]
+        for copy in local[5 + 7 * n:7 + 7 * n]:
+            copy.wait()
+        temb = mm(feats, wtime[:, part])
+        embed = left[0:64, part]
+        emb = embed.astype(F32)
+        gain = gain_ref[:, part]
+        for m, piece in enumerate(split(jnp.concatenate([emb * gain, temb * gain], axis=0))):
+            fold[m * 80:(m + 1) * 80, part] = piece
+        for m, piece in enumerate(split(temb)):
+            left[64 + 16 * m:80 + 16 * m, part] = piece
+        t_row = temb[0:1]
+        right[128:192, part] = embed
+        for copy in local[7 + 7 * n:12 + 7 * n]:
+            copy.wait()
+        right[64:128, part] = right[0:64, part]
+        terms = (
+            jnp.sum(emb * t_row, axis=1, keepdims=True),
+            jnp.sum(t_row * t_row, axis=1, keepdims=True),
+            mm(fold[:, part], wall[part]),
+            lax.dot_general(left[:, part], right[:, part], (((1,), (1,)), ((), ())), preferred_element_type=F32),
+        )
+        for m, term in enumerate(terms):
+            sums[m] = sums[m] + term
+
+    each(0, PARTS - 1, fold_part)
+
     @pl.when(sends_start)
     def _():
         await_bytes(yin.at[0:15], yr)
@@ -229,7 +247,10 @@
     core_rows = pl.ds(pl.multiple_of(128 * c, 128), 128)
     push(zp.at[:, core_rows, :], zp.at[:, core_rows, :], cs, cr, i + 1 - 2 * c, j)
 
-    both = lax.dot_general(left[...], right[...], (((1,), (1,)), ((), ())), preferred_element_type=F32)
+    fold_part(PARTS - 1)
+    twice_et, t_square, folded, both = sums
+    twice_et = 2.0 * twice_et
+    folded = folded[0:80] + folded[80:160]
     cdup = both[0:64, 0:128]
     gram = both[0:64, 128:256]
     mout = both[96:224, 0:128]
@@ -536,7 +557,7 @@
             pltpu.VMEM((LEN, HEAD), BF16),
             pltpu.VMEM((HEAD, LEN), BF16),
             pltpu.VMEM((C + 16, LEN), BF16),
-            dma((14,)),
+            dma((5 + 7 * PARTS,)),
             dma, dma, dma, dma, dma, dma, dma((2,)), dma((2,)),
             dma((2,)), dma((2, 3)), dma((3,)), dma((3,)), dma((3,)), dma((3,)), dma((3,)), dma((3,)), dma, dma,
         ],

time: 73 us -> 72.7 us (level)
  no operation moved by 1% of the time
where the time goes in v8:
time: 72.7 us; the launch traced here: 72.5 us
  Pallas kernels  70.1 us (96%)
  between operations  1.29 us (2%)
  local copies, waits for them, and re-layouts  1.14 us (2%)
    pallas_call x1, Pallas kernels, per_device(): pl.pallas_call(kernel, out_shape=(pltpu.VMEM((2, ROWS, C), F32), pltpu.SM...  70.1 us

profile of v8, /device:TPU:4, one launch (start us, length us, event | category | flops | bytes accessed | tf_op | source)
XLA Modules:
  0.0 72.5 jit_solution(591077076270932849)
XLA Ops:
  1.3 70.1 %shard_map.140 = (f32[2,48,64]{2,1,0:T(8,128)S(1)}, f32[2]{0:T(128)S(4)}) custom-call(s32[1]{0:T(128)S(6)} %copy.19.ws_ref, f32[48,64]{1,0:T(8,128)} %start_hbm.1, bf16[2,48,64]{2,1,0:T(8,128)(2,1)} %noise_hbm.1, f32[1,3072]{1,0:T(1,128)} %bitcast.5, f32[1,128]{1,0:T(1,128)} %bitcast.6, f32[1,128]{1,0:T(1,128)} %bitcast.7, bf16[64,3072]{1,0:T(8,128)(2,1)} %wembed_hbm.1, ...), custom_call_target="tpu_custom_call" | custom-call | tf_op jit(solution)/shard_map/pallas_call | solution.py:514
  71.3 0.6 copy.17
  72.0 0.5 copy.18

commit v9 on v8

--- a/solution.py
+++ b/solution.py
@@ -123,7 +123,16 @@
         pl.semaphore_signal(barrier, inc=1, device_id=(to_i, to_j), device_id_type=MESH)
 
     group(lambda n, ti, tj: greet(ti, tj))
-    column(lambda tj: greet(i, tj))
+    sends_start = lax.rem(y, 2) == c
+    for k in sorted(range(8), key=lambda k: abs(k - 4)):
+        for side in range(2):
+            to_y = c + 2 * side
+            if k:
+                greet(i, 4 * lax.rem(z + k, 8) + to_y)
+            else:
+                @pl.when(y != to_y)
+                def _():
+                    greet(i, 4 * z + to_y)
     base_j = [seq_of(2 * i + n, source_p) for n in range(2)]
     base_mine = [jnp.logical_and(source_i == i, tj == j) for tj in base_j]
     from_j = [first_block + 2 * n for n in range(2)]
@@ -147,7 +156,7 @@
             (wo_hbm.at[pl.ds(head, HEAD), part], left.at[96:224, part]),
         ]
     local = [pltpu.make_async_copy(src, dst, wsem.at[n]) for n, (src, dst) in enumerate(pairs)]
-    for copy in local:
+    for copy in local[:19]:
         copy.start()
 
     local[0].wait()
@@ -159,8 +168,6 @@
     packed_start = jnp.concatenate([
         jnp.where(own_half, pieces[0], pieces[1]), jnp.where(own_half, pieces[2], 0.0)], axis=0).astype(BF16)
     zsrc[...] = packed_start
-    sends_start = lax.rem(y, 2) == c
-
     @pl.when(sends_start)
     def _():
         yin[8 * half + z] = packed_start
@@ -171,11 +178,14 @@
     nin[i] = packed_noise
 
     alone_count = base_mine[0].astype(jnp.int32) + base_mine[1].astype(jnp.int32)
-    pl.semaphore_wait(barrier, 15 + 31 + 2 - alone_count)
+    pl.semaphore_wait(barrier, 15 + 2 - alone_count + 31 * sends_start.astype(jnp.int32))
 
     @pl.when(sends_start)
     def _():
         column(lambda tj: push(zsrc, yin.at[8 * half + z], ys, yr, i, tj))
+
+    for copy in local[19:]:
+        copy.start()
 
 
     first = ws_ref[0]
@@ -267,7 +277,7 @@
     whi = wide.astype(BF16)
     wqkv[:, 0:128] = whi
     wqkv[:, 128:256] = (wide - whi.astype(F32)).astype(BF16)
-    scale_row = qg_ref[...] * kg_ref[...] * (math.log2(math.e) / math.sqrt(HEAD))
+    scale_row = qg_ref[...] * kg_ref[...] * (1.0 / math.sqrt(HEAD))
     scale_col = jnp.broadcast_to(scale_row, (128, 128)).T[:, 0:1]
 
     step_row = lax.broadcasted_iota(jnp.int32, (STEPS, 128), 0)
@@ -325,7 +335,7 @@
         here = slice(keys[0] * KBLK, (keys[-1] + 1) * KBLK)
         scores = [
             mm(kbuf[here], qbuf[:, block * KBLK + side * QBLK:block * KBLK + (side + 1) * QBLK]) for side in range(2)]
-        parts = [mm(vbuf[:, here], jnp.exp2(score).astype(BF16)) for score in scores]
+        parts = [mm(vbuf[:, here], jnp.exp(score).astype(BF16)) for score in scores]
         return [part if acc is None else acc + part for part, acc in zip(parts, accs)]
 
     def finish(lap, block, accs):

time: 72.7 us -> 72.8 us (level)
  no operation moved by 1% of the time
where the time goes in v9:
time: 72.8 us; the launch traced here: 72.5 us
  Pallas kernels  70.1 us (96%)
  between operations  1.29 us (2%)
  local copies, waits for them, and re-layouts  1.14 us (2%)
    pallas_call x1, Pallas kernels, per_device(): pl.pallas_call(kernel, out_shape=(pltpu.VMEM((2, ROWS, C), F32), pltpu.SM...  70.1 us

profile of v9, /device:TPU:4, one launch (start us, length us, event | category | flops | bytes accessed | tf_op | source)
XLA Modules:
  0.0 72.5 jit_solution(7598984376228312579)
XLA Ops:
  1.3 70.1 %shard_map.140 = (f32[2,48,64]{2,1,0:T(8,128)S(1)}, f32[2]{0:T(128)S(4)}) custom-call(s32[1]{0:T(128)S(6)} %copy.19.ws_ref, f32[48,64]{1,0:T(8,128)} %start_hbm.1, bf16[2,48,64]{2,1,0:T(8,128)(2,1)} %noise_hbm.1, f32[1,3072]{1,0:T(1,128)} %bitcast.5, f32[1,128]{1,0:T(1,128)} %bitcast.6, f32[1,128]{1,0:T(1,128)} %bitcast.7, bf16[64,3072]{1,0:T(8,128)(2,1)} %wembed_hbm.1, ...), custom_call_target="tpu_custom_call" | custom-call | tf_op jit(solution)/shard_map/pallas_call | solution.py:524
  71.4 0.6 copy.17
  72.0 0.5 copy.18

commit v10 on v9

--- a/solution.py
+++ b/solution.py
@@ -316,8 +316,8 @@
     low = low_lanes[0:16]
 
     def project(lap, n):
-        packed = latents[lap, n].T
-        zb = jnp.concatenate([packed[0:64], packed[64:128]], axis=1)
+        packed = latents[lap, n].astype(F32).T
+        zb = jnp.concatenate([packed[0:64], packed[64:128]], axis=1).astype(BF16)
         ztr[0:64] = zb
         ztr[128:192] = zb
         cols = slice(n * KBLK, (n + 1) * KBLK)
@@ -328,7 +328,7 @@
         aq = lax.rsqrt(jnp.mean(yq * yq, axis=0, keepdims=True) + EPS * square)
         ak = lax.rsqrt(jnp.mean(yk * yk, axis=0, keepdims=True) + EPS * square)
         qbuf[:, cols] = (yq * aq * scale_col).astype(BF16)
-        kbuf[cols, :] = (yk * ak).astype(BF16).T
+        kbuf[cols, :] = (yk * ak).T.astype(BF16)
         vbuf[0:C, cols] = (yv * lax.rsqrt(square)).astype(BF16)
 
     def attend(block, keys, accs):
@@ -340,7 +340,7 @@
 
     def finish(lap, block, accs):
         outs = [acc[0:C] / acc[C:C + 1] for acc in accs]
-        heads[lap, block] = jnp.concatenate(outs, axis=0).astype(BF16).T
+        heads[lap, block] = jnp.concatenate(outs, axis=0).T.astype(BF16)
         group(lambda n, ti, tj: push(
             heads.at[lap, block, rows_of(n), :], red.at[lap, block, pos], us.at[lap], ur.at[lap, block], ti, tj))
 
@@ -452,11 +452,11 @@
     await_latents(0)
     project(1, 0)
     next_latent(2)
-    to_owners(vpack.at[0], fin0, all_rows, 0)
     await_latents(1)
     project(1, 1)
     early = [attend(block, (0, 1), (None, None)) for block in (0, 1)]
     await_latents(2)
+    to_owners(vpack.at[0], fin0, all_rows, 0)
     project(1, 2)
     for block in (0, 1):
         finish(1, block, attend(block, (2,), early[block]))

time: 72.8 us -> 75.5 us (1.037)
  Pallas kernels: 70.1 us -> 72.9 us
    pallas_call x1, Pallas kernels: 70.1 us -> 72.9 us  [per_device(): pl.pallas_call(kernel, out_shape=(pltpu.VMEM((2, ROWS, C), F32), pltpu.SM...]
where the time goes in v10:
time: 75.5 us; the launch traced here: 75.3 us
  Pallas kernels  72.9 us (97%)
  between operations  1.29 us (2%)
  local copies, waits for them, and re-layouts  1.14 us (2%)
    pallas_call x1, Pallas kernels, per_device(): pl.pallas_call(kernel, out_shape=(pltpu.VMEM((2, ROWS, C), F32), pltpu.SM...  72.9 us

profile of v10, /device:TPU:4, one launch (start us, length us, event | category | flops | bytes accessed | tf_op | source)
XLA Modules:
  0.0 75.3 jit_solution(9735801495156807511)
XLA Ops:
  1.3 72.9 %shard_map.140 = (f32[2,48,64]{2,1,0:T(8,128)S(1)}, f32[2]{0:T(128)S(4)}) custom-call(s32[1]{0:T(128)S(6)} %copy.19.ws_ref, f32[48,64]{1,0:T(8,128)} %start_hbm.1, bf16[2,48,64]{2,1,0:T(8,128)(2,1)} %noise_hbm.1, f32[1,3072]{1,0:T(1,128)} %bitcast.5, f32[1,128]{1,0:T(1,128)} %bitcast.6, f32[1,128]{1,0:T(1,128)} %bitcast.7, bf16[64,3072]{1,0:T(8,128)(2,1)} %wembed_hbm.1, ...), custom_call_target="tpu_custom_call" | custom-call | tf_op jit(solution)/shard_map/pallas_call | solution.py:524
  74.2 0.6 copy.17
  74.8 0.5 copy.18

commit v11 on v8

--- a/solution.py
+++ b/solution.py
@@ -68,9 +68,9 @@
     wtime, wall, fold, left, right, wqkv, cdiag, crow,
     delta_ref, coeff_ref,
     zsrc, yin, nsrc, nin, basesrc, basein,
-    latents, heads, red, vsrc, vpack, gat, zsend, fin0, fin1, first_sums, esrc, ein,
+    latents, heads, red, vsrc, vpack, gat, zsend, fin1, tsend, first_sums, esrc, ein,
     ztr, kbuf, qbuf, vbuf,
-    wsem, ys, yr, cs, cr, ns, nr, bs, br, us, ur, gs, gr, ps, pr, fs, fr, es, er,
+    wsem, ys, yr, cs, cr, ns, nr, bs, br, us, ur, gs, gr, ps, pr, fs, fr, ts, tr, es, er,
 ):
     i = lax.axis_index("step")
     j = lax.axis_index("seq")
@@ -368,7 +368,8 @@
             @pl.when(jnp.logical_and(to_i >= first_i, jnp.logical_not(mine)))
             def _():
                 push(src.at[k % 2, rows], dst.at[s, rows], fs.at[n], fr.at[n], to_i, to_j)
-        each(0, 16, one)
+        for k in reversed(range(16)):
+            one(k)
 
     def owners_sent(dst, rows, n):
         for pair in range(COLS):
@@ -391,9 +392,11 @@
             odd = odd + jnp.where(k == 2 * i + 1, later, 0.0)
         return even, even + odd
 
-    all_rows, early_rows, late_rows = slice(0, 32), slice(0, 16), slice(16, 32)
+    early_rows, late_rows = slice(0, 16), slice(16, 32)
     blocks = range(3)
     velocities = {}
+    through = {}
+    own_delta = jnp.sum(jnp.where(step_row == s, delta, 0.0), axis=0, keepdims=True)
 
     def sum_heads(block):
         velocities[block] = reduce_heads(0, block)
@@ -408,15 +411,32 @@
 
     def next_latent(block):
         rows = slice(block * 16, (block + 1) * 16)
-        latent = jnp.where(low, basein[0, rows], basein[1, rows])
         await_bytes(gat.at[block, 0:STEPS - 1], gr.at[block])
+        before = jnp.zeros((16, 128), F32)
         for n in range(STEPS):
-            latent = latent + jnp.where(n < s, delta_ref[n:n + 1] * gat[block, n].astype(F32), 0.0)
-        latent = latent.astype(BF16)
+            before = before + jnp.where(n < s, delta_ref[n:n + 1] * gat[block, n].astype(F32), 0.0)
+        latent = (jnp.where(low, basein[0, rows], basein[1, rows]) + before).astype(BF16)
         zsend[block] = latent
         latents[1, block, chunk, :] = latent
         group(lambda n, ti, tj: push(
             zsend.at[block], latents.at[1, block, chunk, :], ps.at[block], pr.at[block], ti, tj))
+        through[block] = before + own_delta * vsrc[block].astype(F32)
+
+    def send_through():
+        first_part, second_part, third_part = through[0], through[1], through[2]
+        tsend[0, 0:16] = jnp.where(low, first_part, pltpu.roll(second_part, C, 1))
+        tsend[1, 0:16] = jnp.where(low, pltpu.roll(first_part, C, 1), second_part)
+        tsend[0, 16:32] = jnp.where(low, third_part, 0.0)
+        tsend[1, 16:32] = jnp.where(low, pltpu.roll(third_part, C, 1), 0.0)
+        slot = lax.rem(s, 2)
+        for n in range(2):
+            @pl.when(from_mine[n])
+            def _():
+                first_sums[slot] = tsend[n]
+
+            @pl.when(jnp.logical_not(from_mine[n]))
+            def _():
+                push(tsend.at[n], first_sums.at[slot], ts.at[n], tr.at[slot], from_i, from_j[n])
 
     def await_latents(block):
         await_bytes(latents.at[1, block, 0:15 * 16, :], pr.at[block])
@@ -436,13 +456,11 @@
             await_bytes(basein.at[n], br.at[n])
     next_latent(0)
     next_latent(1)
-    pack_first(0, velocities[0], velocities[1])
-    pack_last(0, velocities[2])
 
     await_latents(0)
     project(1, 0)
     next_latent(2)
-    to_owners(vpack.at[0], fin0, all_rows, 0)
+    send_through()
     await_latents(1)
     project(1, 1)
     early = [attend(block, (0, 1), (None, None)) for block in (0, 1)]
@@ -453,7 +471,10 @@
     finish(1, 2, attend(2, blocks, (None, None)))
     pack_first(1, reduce_heads(1, 0), reduce_heads(1, 1))
     to_owners(vpack.at[1], fin1, early_rows, 1)
-    first_sums[0], first_sums[1] = owner_sums(fin0, all_rows, 0)
+    for n in range(2):
+        @pl.when(jnp.logical_not(base_mine[n]))
+        def _():
+            await_bytes(first_sums.at[n], tr.at[n])
     pack_last(1, reduce_heads(1, 2))
     to_owners(vpack.at[1], fin1, late_rows, 2)
 
@@ -479,7 +500,10 @@
     for block in blocks:
         await_bytes(gat.at[block, 0:STEPS - 1], gs.at[block])
         await_bytes(latents.at[1, block, 0:15 * 16, :], ps.at[block])
-    owners_sent(fin0, all_rows, 0)
+    for n in range(2):
+        @pl.when(jnp.logical_not(from_mine[n]))
+        def _():
+            await_bytes(tsend.at[n], ts.at[n])
     owners_sent(fin1, early_rows, 1)
     owners_sent(fin1, late_rows, 2)
     @pl.when(sends_start)
@@ -549,7 +573,7 @@
             pltpu.VMEM((3, STEPS, 16, 128), BF16),
             pltpu.VMEM((3, 16, 128), BF16),
             pltpu.VMEM((STEPS, 32, 128), BF16),
-            pltpu.VMEM((STEPS, 32, 128), BF16),
+            pltpu.VMEM((2, 32, 128), F32),
             pltpu.VMEM((2, 32, 128), F32),
             pltpu.VMEM((2, 128), F32),
             pltpu.VMEM((SEQ, 2, 128), F32),
@@ -559,7 +583,7 @@
             pltpu.VMEM((C + 16, LEN), BF16),
             dma((5 + 7 * PARTS,)),
             dma, dma, dma, dma, dma, dma, dma((2,)), dma((2,)),
-            dma((2,)), dma((2, 3)), dma((3,)), dma((3,)), dma((3,)), dma((3,)), dma((3,)), dma((3,)), dma, dma,
+            dma((2,)), dma((2, 3)), dma((3,)), dma((3,)), dma((3,)), dma((3,)), dma((3,)), dma((3,)), dma((2,)), dma((2,)), dma, dma,
         ],
         compiler_params=pltpu.CompilerParams(
             collective_id=0, has_side_effects=True, vmem_limit_bytes=56 * 1024 * 1024),

time: 72.7 us -> 72.2 us (level)
  the two profiles are of different devices: /device:TPU:4 before, /device:TPU:1 now
where the time goes in v11:
time: 72.2 us; the launch traced here: 72.1 us
  Pallas kernels  69.7 us (97%)
  between operations  1.29 us (2%)
  local copies, waits for them, and re-layouts  1.14 us (2%)
    pallas_call x1, Pallas kernels, per_device(): pl.pallas_call(kernel, out_shape=(pltpu.VMEM((2, ROWS, C), F32), pltpu.SM...  69.7 us

profile of v11, /device:TPU:1, one launch (start us, length us, event | category | flops | bytes accessed | tf_op | source)
XLA Modules:
  0.0 72.1 jit_solution(17091599674419689416)
XLA Ops:
  1.3 69.7 %shard_map.140 = (f32[2,48,64]{2,1,0:T(8,128)S(1)}, f32[2]{0:T(128)S(4)}) custom-call(s32[1]{0:T(128)S(6)} %copy.19.ws_ref, f32[48,64]{1,0:T(8,128)} %start_hbm.1, bf16[2,48,64]{2,1,0:T(8,128)(2,1)} %noise_hbm.1, f32[1,3072]{1,0:T(1,128)} %bitcast.5, f32[1,128]{1,0:T(1,128)} %bitcast.6, f32[1,128]{1,0:T(1,128)} %bitcast.7, bf16[64,3072]{1,0:T(8,128)(2,1)} %wembed_hbm.1, ...), custom_call_target="tpu_custom_call" | custom-call | tf_op jit(solution)/shard_map/pallas_call | solution.py:538
  71.0 0.6 copy.17
  71.6 0.5 copy.18

commit v12 on v11

--- a/solution.py
+++ b/solution.py
@@ -441,6 +441,7 @@
     def await_latents(block):
         await_bytes(latents.at[1, block, 0:15 * 16, :], pr.at[block])
 
+    send_base()
     await_bytes(zp.at[:, 0:128, :], cr)
     for block in blocks:
         project(0, block)
@@ -448,7 +449,6 @@
         finish(0, block, attend(block, blocks, (None, None)))
         if block:
             sum_heads(block - 1)
-    send_base()
     sum_heads(2)
     for n in range(2):
         @pl.when(jnp.logical_not(from_mine[n]))

time: 72.2 us -> 68.8 us (0.953)
  the two profiles are of different devices: /device:TPU:1 before, /device:TPU:4 now
where the time goes in v12:
time: 68.8 us; the launch traced here: 67.6 us
  Pallas kernels  65.1 us (95%)
  between operations  1.29 us (2%)
  local copies, waits for them, and re-layouts  1.14 us (2%)
    pallas_call x1, Pallas kernels, per_device(): pl.pallas_call(kernel, out_shape=(pltpu.VMEM((2, ROWS, C), F32), pltpu.SM...  65.1 us

profile of v12, /device:TPU:4, one launch (start us, length us, event | category | flops | bytes accessed | tf_op | source)
XLA Modules:
  0.0 67.6 jit_solution(1737460892119189209)
XLA Ops:
  1.3 65.1 %shard_map.140 = (f32[2,48,64]{2,1,0:T(8,128)S(1)}, f32[2]{0:T(128)S(4)}) custom-call(s32[1]{0:T(128)S(6)} %copy.19.ws_ref, f32[48,64]{1,0:T(8,128)} %start_hbm.1, bf16[2,48,64]{2,1,0:T(8,128)(2,1)} %noise_hbm.1, f32[1,3072]{1,0:T(1,128)} %bitcast.5, f32[1,128]{1,0:T(1,128)} %bitcast.6, f32[1,128]{1,0:T(1,128)} %bitcast.7, bf16[64,3072]{1,0:T(8,128)(2,1)} %wembed_hbm.1, ...), custom_call_target="tpu_custom_call" | custom-call | tf_op jit(solution)/shard_map/pallas_call | solution.py:538
  66.4 0.6 copy.17
  67.0 0.5 copy.18

commit v13 on v12

--- a/solution.py
+++ b/solution.py
@@ -449,12 +449,12 @@
         finish(0, block, attend(block, blocks, (None, None)))
         if block:
             sum_heads(block - 1)
-    sum_heads(2)
     for n in range(2):
         @pl.when(jnp.logical_not(from_mine[n]))
         def _():
             await_bytes(basein.at[n], br.at[n])
     next_latent(0)
+    sum_heads(2)
     next_latent(1)
 
     await_latents(0)

time: 68.8 us -> 67.8 us (0.985); the launches traced: 67.6 us -> 67.5 us
  no operation moved by 1% of the time
where the time goes in v13:
time: 67.8 us; the launch traced here: 67.5 us
  Pallas kernels  65.1 us (96%)
  between operations  1.29 us (2%)
  local copies, waits for them, and re-layouts  1.14 us (2%)
    pallas_call x1, Pallas kernels, per_device(): pl.pallas_call(kernel, out_shape=(pltpu.VMEM((2, ROWS, C), F32), pltpu.SM...  65.1 us

profile of v13, /device:TPU:4, one launch (start us, length us, event | category | flops | bytes accessed | tf_op | source)
XLA Modules:
  0.0 67.5 jit_solution(10074434213606535805)
XLA Ops:
  1.3 65.1 %shard_map.140 = (f32[2,48,64]{2,1,0:T(8,128)S(1)}, f32[2]{0:T(128)S(4)}) custom-call(s32[1]{0:T(128)S(6)} %copy.19.ws_ref, f32[48,64]{1,0:T(8,128)} %start_hbm.1, bf16[2,48,64]{2,1,0:T(8,128)(2,1)} %noise_hbm.1, f32[1,3072]{1,0:T(1,128)} %bitcast.5, f32[1,128]{1,0:T(1,128)} %bitcast.6, f32[1,128]{1,0:T(1,128)} %bitcast.7, bf16[64,3072]{1,0:T(8,128)(2,1)} %wembed_hbm.1, ...), custom_call_target="tpu_custom_call" | custom-call | tf_op jit(solution)/shard_map/pallas_call | solution.py:538
  66.4 0.6 copy.17
  67.0 0.5 copy.18
